TPU v7x, 256 devices: a whole 4x4x8 slice. The times are simulated.
256 devices in a mesh: section: 32 (over x, y, core), dp: 8 (over z).
Axes of the slice: x: 4, y: 4, z: 8, core: 2. Of those that a mesh axis runs over, the one named last changes fastest.
Arguments:
- inputs: bfloat16 [8, 128, 2560], P('dp'), may hold values from -6 to 6
- span_lengths: int32 [8, 8], P('dp'), may hold values from 1 to 20, 128 in all within a row
- qkv_weight: bfloat16 [32, 2560, 3840], P('section', 'dp'), may hold values from -0.125 to 0.125
- out_weight: bfloat16 [32, 2560, 1280], P('section', 'dp'), may hold values from -0.25 to 0.25
Outputs:
- hidden_out: bfloat16 [8, 128, 2560], P('dp', 'section')
Inputs may be any that keep to these rules, and one draw needn't show every extreme that they name: `span_lengths`: each row sums to 128, and its largest entry is exactly 20.
All inputs are finite; a program needn't handle non-finite values.
Results may differ from a plain program's by a relative error of at most 0.027.
Values may be sent and summed in bfloat16 or wider, within the bound.
A program may use at most 128 MiB of HBM per device.

v0:
```python
import jax
import jax.numpy as jnp
from jax import lax
from jax.sharding import PartitionSpec as P

HD = 128
GROUP = 4
SPANS = 8
LEN = 128
CMAX = 20


def from_partner(block, axis, apart):
    count = lax.axis_size(axis)
    route = []
    for low in range(count):
        high = low | 1 << apart
        if high != low and high < count:
            route += [(low, high), (high, low)]
    return lax.ppermute(block, axis, route)


def from_behind(array, axis, by):
    devices = lax.axis_size(axis)
    pairs = [(i, i + by) for i in range(devices) if 0 <= i + by < devices]
    return lax.ppermute(array, axis, pairs)


def spread(array, axis, root):
    mine = lax.axis_index(axis) == root
    return lax.psum(jnp.where(mine, array, jnp.zeros_like(array)), axis)


def layer_norm(hidden):
    values = hidden.astype(jnp.float32)
    row_mean = jnp.mean(values, axis=-1, keepdims=True)
    centred = values - row_mean
    row_var = jnp.mean(centred * centred, axis=-1, keepdims=True)
    return (centred * lax.rsqrt(row_var + 1e-05)).astype(jnp.bfloat16)


def pick_entry(table, wanted):
    seg_ids = jnp.arange(table.shape[0], dtype=jnp.int32)
    return jnp.sum(jnp.where(seg_ids == wanted, table, 0), dtype=jnp.int32)


def shards(inputs, span_lengths, qkv_weight, out_weight):
    section_count = lax.axis_size("section")
    layer_count = section_count // GROUP
    section_index = lax.axis_index("section")
    layer_index = section_index // GROUP
    qkv_full, out_full = (
        lax.all_gather(qkv_weight, "dp", axis=1, tiled=True),
        lax.all_gather(out_weight, "dp", axis=1, tiled=True),
    )
    qkv_mat = qkv_full[0]
    out_mat = out_full[0]
    width = qkv_mat.shape[0]
    head_cols = out_mat.shape[1]
    heads_dev = head_cols // HD
    scale = HD ** (-0.5)
    seg_lengths = span_lengths[0]
    seg_ends = jnp.cumsum(seg_lengths)
    seg_starts = seg_ends - seg_lengths
    sequence = inputs[0]
    padded_in = jnp.concatenate([sequence, jnp.zeros((CMAX, width), jnp.bfloat16)], 0)

    def attend(h_in, key_cache, value_cache, seg_start, key_start):
        normed = layer_norm(h_in)
        projected = jnp.dot(normed, qkv_mat, preferred_element_type=jnp.float32).astype(
            jnp.bfloat16
        )
        queries = projected[:, :head_cols]
        key_cache = lax.dynamic_update_slice(
            key_cache, projected[:, head_cols : 2 * head_cols], (seg_start, 0)
        )
        value_cache = lax.dynamic_update_slice(
            value_cache, projected[:, 2 * head_cols :], (seg_start, 0)
        )
        key_block = lax.dynamic_slice(key_cache, (key_start, 0), (2 * CMAX, head_cols))
        value_block = lax.dynamic_slice(value_cache, (key_start, 0), (2 * CMAX, head_cols))
        query_heads = queries.reshape(CMAX, heads_dev, HD)
        key_heads = key_block.reshape(2 * CMAX, heads_dev, HD)
        value_heads = value_block.reshape(2 * CMAX, heads_dev, HD)
        scores = (
            jnp.einsum("qhe,khe->hqk", query_heads, key_heads, preferred_element_type=jnp.float32)
            * scale
        )
        query_pos = seg_start + jnp.arange(CMAX, dtype=jnp.int32)
        key_pos = key_start + jnp.arange(2 * CMAX, dtype=jnp.int32)
        allowed = key_pos[None, :] <= query_pos[:, None]
        weights = jnp.where(allowed[None], jnp.exp(scores), 0.0)
        probs = (weights / jnp.sum(weights, axis=-1, keepdims=True)).astype(jnp.bfloat16)
        attended = jnp.einsum(
            "hqk,khe->qhe", probs, value_heads, preferred_element_type=jnp.float32
        )
        return (attended.astype(jnp.bfloat16).reshape(CMAX, head_cols), key_cache, value_cache)

    def spare(h_in, key_cache, value_cache, seg_start, key_start):
        return (jnp.zeros((CMAX, head_cols), jnp.bfloat16), key_cache, value_cache)

    def advance(step_index, carry):
        incoming, key_cache, value_cache, finished = carry
        seg_raw = step_index - layer_index
        active = (seg_raw >= 0) & (seg_raw < SPANS)
        seg_index = jnp.clip(seg_raw, 0, SPANS - 1)
        seg_start = pick_entry(seg_starts, seg_index)
        key_start = pick_entry(seg_starts, jnp.maximum(seg_index - 1, 0))
        from_input = lax.dynamic_slice(padded_in, (seg_start, 0), (CMAX, width))
        h_in = jnp.where(layer_index == 0, from_input, incoming)
        attended, key_cache, value_cache = lax.cond(
            active, attend, spare, h_in, key_cache, value_cache, seg_start, key_start
        )
        partial_value = lax.dot_general(
            attended, out_mat, (((1,), (1,)), ((), ())), preferred_element_type=jnp.float32
        )
        summed = partial_value + from_partner(
            partial_value.astype(jnp.bfloat16), "section", 0
        ).astype(partial_value.dtype)
        summed = summed + from_partner(summed.astype(jnp.bfloat16), "section", 1).astype(
            summed.dtype
        )
        h_out = (h_in.astype(jnp.float32) + summed).astype(jnp.bfloat16)
        old_slot = lax.dynamic_slice(finished, (seg_start, 0), (CMAX, width))
        new_slot = jnp.where(active & (layer_index == layer_count - 1), h_out, old_slot)
        finished = lax.dynamic_update_slice(finished, new_slot, (seg_start, 0))
        incoming = from_behind(h_out, "section", GROUP)
        return (incoming, key_cache, value_cache, finished)

    start_carry = (
        jnp.zeros((CMAX, width), jnp.bfloat16),
        jnp.zeros((LEN + 2 * CMAX, head_cols), jnp.bfloat16),
        jnp.zeros((LEN + 2 * CMAX, head_cols), jnp.bfloat16),
        jnp.zeros((LEN + CMAX, width), jnp.bfloat16),
    )
    carry = lax.fori_loop(0, layer_count + SPANS - 1, advance, start_carry)
    finished = carry[3]
    result = spread(finished[:LEN], "section", section_count - 1)
    row_count = LEN // section_count
    own_rows = lax.dynamic_slice(result, (section_index * row_count, 0), (row_count, width))
    return own_rows[None]


def solution(mesh):
    in_specs = (
        P("dp", None, None),
        P("dp", None),
        P("section", "dp", None),
        P("section", "dp", None),
    )
    out_specs = P("dp", "section", None)
    return jax.shard_map(shards, mesh=mesh, in_specs=in_specs, out_specs=out_specs, check_vma=False)
```

profile of v0, /device:TPU:23, one launch (start us, length us, event | category | flops | bytes accessed | tf_op | source)
XLA Modules:
  0.0 1006.8 jit_solution(8198509974102716253)
XLA Ops:
  10.7 78.1 %all-gather.5.cloned.1.call-done = bf16[1,2560,1280]{2,1,0:T(8,128)(2,1)} async-done(((bf16[1,320,1280]{2,1,0:T(8,128)(2,1)}), bf16[1,2560,1280]{2,1,0:T(8,128)(2,1)}) %all-gather.5.cloned.1.call-update) | async-done | bytes 6553616 | tf_op jit(solution)/shard_map/all_gather | solution.py:54
  88.8 200.2 %all-gather.3.cloned.1.call-done = bf16[1,2560,3840]{2,1,0:T(8,128)(2,1)} async-done(((bf16[1,320,3840]{2,1,0:T(8,128)(2,1)}), bf16[1,2560,3840]{2,1,0:T(8,128)(2,1)}) %all-gather.3.cloned.1.call-update) | async-done | bytes 19660816 | tf_op jit(solution)/shard_map/all_gather | solution.py:53
  289.2 597.0 %while.21 = (s32[]{:T(128)}, bf16[20,2560]{1,0:T(8,128)(2,1)S(1)}, bf16[168,1280]{1,0:T(8,128)(2,1)S(1)}, bf16[168,1280]{1,0:T(8,128)(2,1)S(1)}, bf16[148,2560]{...) while((s32[]{:T(128)}, bf16[20,2560]{1,0:T(8,128)(2,1)S(1)}, ...), condition=%wide.region_9.10_spmd, body=%wide.region_1.9_spmd.sunk | while | flops 529697184 | bytes 31739944 | solution.py:136
  291.9 4.7 fusion.35
  299.3 3.6 collective-permute-done.1
  305.5 4.7 collective-permute-done.2
  312.8 4.7 fusion.35
  321.8 3.6 collective-permute-done.1
  328.0 4.7 collective-permute-done.2
  335.3 4.7 fusion.35
  344.4 3.6 collective-permute-done.1
  350.6 4.7 collective-permute-done.2
  357.9 4.7 fusion.35
  366.9 3.6 collective-permute-done.1
  373.1 4.7 collective-permute-done.2
  380.5 4.7 fusion.35
  395.8 5.4 collective-permute-done.2
  403.9 4.7 fusion.35
  413.5 3.4 collective-permute-done.1
  419.5 5.2 collective-permute-done.2
  427.4 4.7 fusion.35
  437.0 3.4 collective-permute-done.1
  443.0 114.2 %collective-permute-done.2 = bf16[20,2560]{1,0:T(8,128)(2,1)S(1)} collective-permute-done((bf16[20,2560]{1,0:T(8,128)(2,1)S(1)}, bf16[20,2560]{1,0:T(8,128)(2,1)S(1)}, u32[]{:S(2)}, u32[]{:S(2)}) %collective-permute-start.2) | collective-permute-done | bytes 102432 | tf_op jit(solution)/shard_map/while/body/eval_jaxpr/ppermute | solution.py:26
  559.8 17.9 %conditional.2 = (bf16[20,1280]{1,0:T(8,128)(2,1)S(1)}, bf16[168,1280]{1,0:T(8,128)(2,1)S(1)}, bf16[168,1280]{1,0:T(8,128)(2,1)S(1)}) conditional(s32[]{:T(128)} %convert_element_type.138, (bf16[168,1280]{1,0:T(8,128)(2,1)S(1)}, bf16[168,1280]{1,0:T(8,128)(2,1)S(1)}) %tuple.62, (bf16[20,2560]{1,0:T(8,128)(2,1)S(1)}, bf16[2560,3840]{1,0:T(8,128)(2,1)}, ...), branch_computations={%region_3.3_spmd, %region_4.8_spmd} | conditional | flops 397959552 | bytes 21857758 | solution.py:111
  560.2 9.3 convolution_convert_fusion
  577.7 4.7 fusion.35
  586.7 3.4 collective-permute-done.1
  592.6 5.9 collective-permute-done.2
  601.1 17.9 %conditional.2 = (bf16[20,1280]{1,0:T(8,128)(2,1)S(1)}, bf16[168,1280]{1,0:T(8,128)(2,1)S(1)}, bf16[168,1280]{1,0:T(8,128)(2,1)S(1)}) conditional(s32[]{:T(128)} %convert_element_type.138, (bf16[168,1280]{1,0:T(8,128)(2,1)S(1)}, bf16[168,1280]{1,0:T(8,128)(2,1)S(1)}) %tuple.62, (bf16[20,2560]{1,0:T(8,128)(2,1)S(1)}, bf16[2560,3840]{1,0:T(8,128)(2,1)}, ...), branch_computations={%region_3.3_spmd, %region_4.8_spmd} | conditional | flops 397959552 | bytes 21857758 | solution.py:111
  601.5 9.3 convolution_convert_fusion
  619.0 4.7 fusion.35
  628.0 3.4 collective-permute-done.1
  633.9 5.8 collective-permute-done.2
  642.4 17.9 %conditional.2 = (bf16[20,1280]{1,0:T(8,128)(2,1)S(1)}, bf16[168,1280]{1,0:T(8,128)(2,1)S(1)}, bf16[168,1280]{1,0:T(8,128)(2,1)S(1)}) conditional(s32[]{:T(128)} %convert_element_type.138, (bf16[168,1280]{1,0:T(8,128)(2,1)S(1)}, bf16[168,1280]{1,0:T(8,128)(2,1)S(1)}) %tuple.62, (bf16[20,2560]{1,0:T(8,128)(2,1)S(1)}, bf16[2560,3840]{1,0:T(8,128)(2,1)}, ...), branch_computations={%region_3.3_spmd, %region_4.8_spmd} | conditional | flops 397959552 | bytes 21857758 | solution.py:111
  642.8 9.3 convolution_convert_fusion
  660.2 4.7 fusion.35
  669.2 3.4 collective-permute-done.1
  675.2 5.8 collective-permute-done.2
  683.6 17.9 %conditional.2 = (bf16[20,1280]{1,0:T(8,128)(2,1)S(1)}, bf16[168,1280]{1,0:T(8,128)(2,1)S(1)}, bf16[168,1280]{1,0:T(8,128)(2,1)S(1)}) conditional(s32[]{:T(128)} %convert_element_type.138, (bf16[168,1280]{1,0:T(8,128)(2,1)S(1)}, bf16[168,1280]{1,0:T(8,128)(2,1)S(1)}) %tuple.62, (bf16[20,2560]{1,0:T(8,128)(2,1)S(1)}, bf16[2560,3840]{1,0:T(8,128)(2,1)}, ...), branch_computations={%region_3.3_spmd, %region_4.8_spmd} | conditional | flops 397959552 | bytes 21857758 | solution.py:111
  684.0 9.3 convolution_convert_fusion
  701.5 4.7 fusion.35
  710.5 3.4 collective-permute-done.1
  716.4 5.8 collective-permute-done.2
  724.9 17.9 %conditional.2 = (bf16[20,1280]{1,0:T(8,128)(2,1)S(1)}, bf16[168,1280]{1,0:T(8,128)(2,1)S(1)}, bf16[168,1280]{1,0:T(8,128)(2,1)S(1)}) conditional(s32[]{:T(128)} %convert_element_type.138, (bf16[168,1280]{1,0:T(8,128)(2,1)S(1)}, bf16[168,1280]{1,0:T(8,128)(2,1)S(1)}) %tuple.62, (bf16[20,2560]{1,0:T(8,128)(2,1)S(1)}, bf16[2560,3840]{1,0:T(8,128)(2,1)}, ...), branch_computations={%region_3.3_spmd, %region_4.8_spmd} | conditional | flops 397959552 | bytes 21857758 | solution.py:111
  725.3 9.3 convolution_convert_fusion
  742.8 4.7 fusion.35
  751.8 3.4 collective-permute-done.1
  757.7 5.8 collective-permute-done.2
  766.2 17.9 %conditional.2 = (bf16[20,1280]{1,0:T(8,128)(2,1)S(1)}, bf16[168,1280]{1,0:T(8,128)(2,1)S(1)}, bf16[168,1280]{1,0:T(8,128)(2,1)S(1)}) conditional(s32[]{:T(128)} %convert_element_type.138, (bf16[168,1280]{1,0:T(8,128)(2,1)S(1)}, bf16[168,1280]{1,0:T(8,128)(2,1)S(1)}) %tuple.62, (bf16[20,2560]{1,0:T(8,128)(2,1)S(1)}, bf16[2560,3840]{1,0:T(8,128)(2,1)}, ...), branch_computations={%region_3.3_spmd, %region_4.8_spmd} | conditional | flops 397959552 | bytes 21857758 | solution.py:111
  766.6 9.3 convolution_convert_fusion
  784.0 4.7 fusion.35
  793.1 3.4 collective-permute-done.1
  799.0 5.8 collective-permute-done.2
  807.5 17.9 %conditional.2 = (bf16[20,1280]{1,0:T(8,128)(2,1)S(1)}, bf16[168,1280]{1,0:T(8,128)(2,1)S(1)}, bf16[168,1280]{1,0:T(8,128)(2,1)S(1)}) conditional(s32[]{:T(128)} %convert_element_type.138, (bf16[168,1280]{1,0:T(8,128)(2,1)S(1)}, bf16[168,1280]{1,0:T(8,128)(2,1)S(1)}) %tuple.62, (bf16[20,2560]{1,0:T(8,128)(2,1)S(1)}, bf16[2560,3840]{1,0:T(8,128)(2,1)}, ...), branch_computations={%region_3.3_spmd, %region_4.8_spmd} | conditional | flops 397959552 | bytes 21857758 | solution.py:111
  807.8 9.3 convolution_convert_fusion
  825.3 4.7 fusion.35
  834.3 3.4 collective-permute-done.1
  840.3 5.8 collective-permute-done.2
  848.7 17.9 %conditional.2 = (bf16[20,1280]{1,0:T(8,128)(2,1)S(1)}, bf16[168,1280]{1,0:T(8,128)(2,1)S(1)}, bf16[168,1280]{1,0:T(8,128)(2,1)S(1)}) conditional(s32[]{:T(128)} %convert_element_type.138, (bf16[168,1280]{1,0:T(8,128)(2,1)S(1)}, bf16[168,1280]{1,0:T(8,128)(2,1)S(1)}) %tuple.62, (bf16[20,2560]{1,0:T(8,128)(2,1)S(1)}, bf16[2560,3840]{1,0:T(8,128)(2,1)}, ...), branch_computations={%region_3.3_spmd, %region_4.8_spmd} | conditional | flops 397959552 | bytes 21857758 | solution.py:111
  849.1 9.3 convolution_convert_fusion
  866.6 4.7 fusion.35
  875.6 3.4 collective-permute-done.1
  881.5 4.7 collective-permute-done.2
  887.1 111.8 %all-reduce.3.cloned.1.call-done = bf16[128,2560]{1,0:T(8,128)(2,1)} async-done(((bf16[128,2560]{1,0:T(8,128)(2,1)}), bf16[128,2560]{1,0:T(8,128)(2,1)}) %all-reduce.3.cloned.1.call-update) | async-done | bytes 655376 | tf_op jit(solution)/shard_map/psum | solution.py:31
  (339 shorter events, 159.9 us)
Async XLA Ops:
  6.5 82.3 %all-gather.5.cloned.1.call-start = ((), (), s32[]{:S(2)}) async-start(), calls=%async_computation.1 | async-start | bytes 7372800 | tf_op jit(solution)/shard_map/all_gather | solution.py:54
  7.3 281.8 %all-gather.3.cloned.1.call-start = ((), (), s32[]{:S(2)}) async-start(), calls=%async_computation | async-start | bytes 22118400 | tf_op jit(solution)/shard_map/all_gather | solution.py:53
  8.0 990.9 %all-reduce.3.cloned.1.call-start = ((), (), s32[]{:S(2)}) async-start(), calls=%async_computation.2 | async-start | bytes 1310720 | tf_op jit(solution)/shard_map/psum | solution.py:31
  296.6 1.7 collective-permute-start
  298.3 4.6 collective-permute-start.1
  303.0 7.1 collective-permute-start.2
  317.4 3.3 collective-permute-start
  320.8 4.6 collective-permute-start.1
  325.5 7.1 collective-permute-start.2
  340.0 3.3 collective-permute-start
  343.4 4.6 collective-permute-start.1
  348.1 7.1 collective-permute-start.2
  362.6 3.3 collective-permute-start
  365.9 4.6 collective-permute-start.1
  370.7 7.1 collective-permute-start.2
  385.1 3.3 collective-permute-start
  388.5 4.7 collective-permute-start.1
  393.3 7.9 collective-permute-start.2
  408.6 3.1 collective-permute-start
  411.6 5.3 collective-permute-start.1
  417.0 7.6 collective-permute-start.2
  432.0 3.1 collective-permute-start
  435.1 5.3 collective-permute-start.1
  440.5 116.7 %collective-permute-start.2 = (bf16[20,2560]{1,0:T(8,128)(2,1)S(1)}, bf16[20,2560]{1,0:T(8,128)(2,1)S(1)}, u32[]{:S(2)}, u32[]{:S(2)}) collective-permute-start(bf16[20,2560]{1,0:T(8,128)(2,1)S(1)} %get-tuple-element.474), channel_id=1, source_target_pairs={{0,32},{8,40},{16,48},{24,56},{32,64},{40,72},{48,80},{56,88},{64,... | collective-permute-start | bytes 307208 | tf_op jit(solution)/shard_map/while/body/eval_jaxpr/ppermute | solution.py:26
  582.3 3.1 collective-permute-start
  585.4 4.6 collective-permute-start.1
  590.2 8.3 collective-permute-start.2
  623.6 3.1 collective-permute-start
  626.7 4.6 collective-permute-start.1
  631.4 8.3 collective-permute-start.2
  664.9 3.1 collective-permute-start
  668.0 4.6 collective-permute-start.1
  672.7 8.3 collective-permute-start.2
  706.1 3.1 collective-permute-start
  709.2 4.6 collective-permute-start.1
  714.0 8.3 collective-permute-start.2
  747.4 3.1 collective-permute-start
  750.5 4.6 collective-permute-start.1
  755.2 8.3 collective-permute-start.2
  788.7 3.1 collective-permute-start
  791.8 4.6 collective-permute-start.1
  796.5 8.3 collective-permute-start.2
  830.0 3.1 collective-permute-start
  833.1 4.6 collective-permute-start.1
  837.8 8.3 collective-permute-start.2
  871.2 3.1 collective-permute-start
  874.3 4.6 collective-permute-start.1
  879.1 7.1 collective-permute-start.2
Sparse Core Ops, SparseCore 0:
  9.1 79.6 all-gather.4
  90.6 198.3 all-gather.2
  887.2 111.6 all-reduce.2
where the time goes:
time: 1010 us
  waiting for transfers between devices  647 us (64%)
  matrix products  148 us (15%)
  starting transfers between devices  70.1 us (7%)
  loops' own time  62.2 us (6%)
  other arithmetic  34.5 us (3%)
  local copies, waits for them, and re-layouts  32.5 us (3%)
  between operations  13.2 us (1%)
    all_gather x1, waiting for transfers between devices, shards(): lax.all_gather(qkv_weight, 'dp', axis=1, tiled=True)  200 us
    ppermute x15, waiting for transfers between devices, from_behind(): return lax.ppermute(array, axis, pairs)  189 us
    psum x1, waiting for transfers between devices, spread(): return lax.psum(jnp.where(mine, array, jnp.zeros_like(array)), axis)  112 us
    all_gather x1, waiting for transfers between devices, shards(): lax.all_gather(out_weight, 'dp', axis=1, tiled=True)  78.1 us
    dot_general x8, matrix products, attend(): jnp.dot(normed, qkv_mat, preferred_element_type=jnp.float32)  74.7 us
    dot_general x15, matrix products, advance(): lax.dot_general(attended, out_mat, (((1,), (1,)), ((), ())), preferred_el...  69.8 us
    ppermute x30, waiting for transfers between devices, from_partner(): return lax.ppermute(block, axis, route)  65.9 us
    ppermute x30, starting transfers between devices, from_partner(): return lax.ppermute(block, axis, route)  50.6 us
  transfers between devices with their start and end apart: 48, of which 48 were waited for; matrix products, arithmetic and copies ran while one was open for 2% of the time, Pallas kernels for 0%

commit v1 on v0

v1 whole, which is shorter than its diff:
```python
import jax
import jax.numpy as jnp
from jax import lax
from jax.experimental import pallas as pl
from jax.experimental.pallas import tpu as pltpu
from jax.sharding import PartitionSpec as P

HD = 128
GROUP = 4
SPANS = 8
LEN = 128
DP = 8
WIDTH = 2560
ROWS = 320
SLOTS = 5
CHUNK = 16
CHUNKS = LEN // CHUNK
BACK = 48
KEYS = BACK + CHUNK
PIECE = 640
MESH = pl.DeviceIdType.MESH


def kernel(
    x_ref, ks_ref, qkv_ref, ow_ref, out_ref,
    w, hbuf, normed, kc, vc, ksb, part, sendb, rbuf, hnew, outb,
    sem_w, sem_z, sem_x, sem_y, sem_yx, sem_c, sem_c2, sem_cx,
    snd_y, snd_yx, snd_c, snd_c2, snd_cx,
    sem_k, snd_k, sem_h, snd_i, sem_r, snd_r, snd_h, sem_o,
):
    sec = lax.axis_index("section")
    z = lax.axis_index("dp")
    layers = lax.axis_size("section") // GROUP
    layer = sec // GROUP
    g = sec % GROUP
    base = layer * GROUP
    y_mate = base + (g + 2) % GROUP
    slot_y = (g + 2) % GROUP
    core = g % 2
    mate = g + 1 - 2 * core
    c_mate = base + mate
    slot_cy = (mate + 2) % GROUP
    zg = z % GROUP
    own_seq = z // 2 == g

    def remote(src, dst, s_sem, r_sem, to_sec, to_z):
        return pltpu.make_async_remote_copy(
            src_ref=src, dst_ref=dst, send_sem=s_sem, recv_sem=r_sem,
            device_id=(to_sec, to_z), device_id_type=MESH,
        )

    def drain(ref, sem):
        pltpu.make_async_copy(ref, ref, sem).wait()

    @pl.when(own_seq)
    def _():
        e = z % 2
        pltpu.make_async_copy(ks_ref, ksb.at[e], sem_k).start()
        for d in range(1, DP):
            remote(ks_ref, ksb.at[e], snd_k.at[d - 1], sem_k, sec, (z + d) % DP).start()

    feeds = own_seq & (layer == 0)

    def feed(c):
        e = z % 2
        src = x_ref.at[0, pl.ds(pl.multiple_of(c * CHUNK, CHUNK), CHUNK), :]
        dst = hbuf.at[c, pl.ds(pl.multiple_of(e * CHUNK, CHUNK), CHUNK), :]
        pltpu.make_async_copy(src, dst, sem_h.at[c]).start()
        for d in range(1, DP):
            remote(src, dst, snd_i.at[c], sem_h.at[c], sec, (z + d) % DP).start()

    @pl.when(feeds)
    def _():
        feed(0)

    def parts(i, slot):
        rows = pl.ds(pl.multiple_of(z * ROWS, ROWS), ROWS)
        col = lambda n: pl.ds(pl.multiple_of(n * HD, HD), HD)
        out = []
        for p in range(3):
            out.append((qkv_ref.at[0, :, col(10 * p + i)], w.at[slot, rows, pl.ds(HD * p, HD)]))
        out.append((ow_ref.at[0, :, col(i)], w.at[slot, rows, pl.ds(3 * HD, HD)]))
        return out

    def send_head(i, to_z, slot, d, s_sem, r_sem):
        @pl.when(to_z == z)
        def _():
            for src, dst in parts(i, slot):
                pltpu.make_async_copy(src, dst, r_sem.at[0]).start()

        @pl.when(to_z != z)
        def _():
            for src, dst in parts(i, slot):
                remote(src, dst, s_sem, r_sem.at[d], sec, to_z).start()

    def spread(n, _):
        k = lax.rem(n, 2)
        d = (1 - 2 * k) * ((n + 1) // 2)
        d = (d + DP) % DP
        to_z = (z + d) % DP
        send_head(to_z, to_z, g, d, sem_w.at[n], sem_z)

        @pl.when((to_z == g) | (to_z == g + GROUP))
        def _():
            m = to_z // GROUP
            send_head(8 + m, to_z, 4, d, sem_w.at[DP + m], sem_x)

        return 0

    lax.fori_loop(0, DP, spread, 0)

    def block(slot, d):
        return w.at[slot, pl.ds(pl.multiple_of((z + DP - d) % DP * ROWS, ROWS), ROWS), :]

    def order(n):
        k = lax.rem(n, 2)
        return ((1 - 2 * k) * ((n + 1) // 2) + DP) % DP

    def relay(n, _):
        @pl.when(n < DP)
        def _():
            d = order(n)
            drain(block(g, d), sem_z.at[d])
            b = block(g, d)
            remote(b, b, snd_y.at[d], sem_y.at[d], y_mate, z).start()
            remote(b, b, snd_c.at[d], sem_c.at[d], c_mate, z).start()

            @pl.when(zg == g)
            def _():
                x = block(4, d)
                drain(x, sem_x.at[d])
                remote(x, x, snd_yx.at[d], sem_yx.at[d], y_mate, z).start()
                remote(x, x, snd_cx.at[d], sem_cx.at[d], c_mate, z).start()

        @pl.when(n > 0)
        def _():
            d = order(n - 1)
            b = block(slot_y, d)
            drain(b, sem_y.at[d])
            remote(b, b, snd_c2.at[d], sem_c2.at[d], c_mate, z).start()

            @pl.when(zg == slot_y)
            def _():
                x = block(4, d)
                drain(x, sem_yx.at[d])
                remote(x, x, snd_cx.at[d], sem_cx.at[d], c_mate, z).start()

        return 0

    lax.fori_loop(0, DP + 1, relay, 0)

    kc[:, pl.ds(0, BACK), :] = jnp.zeros((2, BACK, SLOTS * HD), jnp.bfloat16)
    vc[:, pl.ds(0, BACK), :] = jnp.zeros((2, BACK, SLOTS * HD), jnp.bfloat16)

    def arrive(n, _):
        d = order(n)
        drain(block(mate, d), sem_c.at[d])
        drain(block(slot_cy, d), sem_c2.at[d])

        @pl.when((zg == mate) | (zg == slot_cy))
        def _():
            drain(block(4, d), sem_cx.at[d])

        return 0

    lax.fori_loop(0, DP, arrive, 0)
    drain(ksb, sem_k)

    e_own = z // GROUP
    cc_own = z % GROUP
    row_own = pl.ds(pl.multiple_of(e_own * CHUNK, CHUNK), CHUNK)
    col_own = pl.ds(pl.multiple_of(cc_own * PIECE, PIECE), PIECE)
    scale = HD ** (-0.5)
    last = layer == layers - 1

    def step(c, _):
        @pl.when(feeds & (c < CHUNKS - 1))
        def _():
            feed(c + 1)

        drain(hbuf.at[c], sem_h.at[c])
        values = hbuf[c].astype(jnp.float32)
        mean = jnp.mean(values, axis=-1, keepdims=True)
        centred = values - mean
        var = jnp.mean(centred * centred, axis=-1, keepdims=True)
        normed[...] = (centred * lax.rsqrt(var + 1e-05)).astype(jnp.bfloat16)

        def project(cols):
            mat = [w[s, :, pl.ds(p * HD, HD * n)] for s, p, n in cols]
            mat = mat[0] if len(mat) == 1 else jnp.concatenate(mat, axis=1)
            return jnp.dot(normed[...], mat, preferred_element_type=jnp.float32).astype(jnp.bfloat16)

        new = pl.ds(pl.multiple_of(c * CHUNK + BACK, CHUNK), CHUNK)
        queries = []
        for s in range(SLOTS):
            qk = project([(s, 0, 2)])
            queries.append(qk[:, :HD])
            kc[0, new, pl.ds(s * HD, HD)] = qk[:CHUNK, HD:]
            kc[1, new, pl.ds(s * HD, HD)] = qk[CHUNK:, HD:]
        for s in (0, 2, 4):
            n = 2 if s < 4 else 1
            v = project([(s + i, 2, 1) for i in range(n)])
            vc[0, new, pl.ds(s * HD, n * HD)] = v[:CHUNK]
            vc[1, new, pl.ds(s * HD, n * HD)] = v[CHUNK:]

        tok = pl.ds(pl.multiple_of(c * CHUNK, CHUNK), CHUNK)
        first = jnp.concatenate([ksb[0, tok, :], ksb[1, tok, :]], axis=0).astype(jnp.float32)
        row = lax.broadcasted_iota(jnp.int32, (2 * CHUNK, 2 * KEYS), 0)
        col = lax.broadcasted_iota(jnp.int32, (2 * CHUNK, 2 * KEYS), 1)
        same = (row < CHUNK) == (col < KEYS)
        key_pos = c * CHUNK - BACK + jnp.where(col < KEYS, col, col - KEYS)
        tok_pos = c * CHUNK + jnp.where(row < CHUNK, row, row - CHUNK)
        allowed = same & (key_pos <= tok_pos) & (key_pos.astype(jnp.float32) >= first)

        window = pl.ds(pl.multiple_of(c * CHUNK, CHUNK), KEYS)
        attended = []
        for s in range(SLOTS):
            cols = pl.ds(s * HD, HD)
            keys = jnp.concatenate([kc[0, window, cols], kc[1, window, cols]], axis=0)
            vals = jnp.concatenate([vc[0, window, cols], vc[1, window, cols]], axis=0)
            scores = lax.dot_general(
                queries[s], keys, (((1,), (1,)), ((), ())), preferred_element_type=jnp.float32
            ) * scale
            weights = jnp.where(allowed, jnp.exp(scores), 0.0)
            probs = (weights / jnp.sum(weights, axis=-1, keepdims=True)).astype(jnp.bfloat16)
            attended.append(
                jnp.dot(probs, vals, preferred_element_type=jnp.float32).astype(jnp.bfloat16)
            )

        for cc in range(GROUP):
            total = None
            rows = pl.ds(cc * PIECE, PIECE)
            for s in (0, 2, 4):
                n = 2 if s < 4 else 1
                lhs = attended[s] if n == 1 else jnp.concatenate(attended[s : s + n], axis=1)
                rhs = [w[s + i, rows, pl.ds(3 * HD, HD)] for i in range(n)]
                rhs = rhs[0] if n == 1 else jnp.concatenate(rhs, axis=1)
                term = lax.dot_general(
                    lhs, rhs, (((1,), (1,)), ((), ())), preferred_element_type=jnp.float32
                )
                total = term if total is None else total + term
            cols = pl.ds(cc * PIECE, PIECE)
            part[:, cols] = total
            sendb[c, :, cols] = total.astype(jnp.bfloat16)
            for e in range(2):
                to_z = e * GROUP + cc

                @pl.when(z != to_z)
                def _():
                    d = (to_z - z + DP) % DP
                    remote(
                        sendb.at[c, pl.ds(e * CHUNK, CHUNK), cols], rbuf.at[c, d - 1],
                        snd_r.at[c], sem_r.at[c], sec, to_z,
                    ).start()

        total = part[row_own, col_own] + hbuf[c, row_own, col_own].astype(jnp.float32)
        drain(rbuf.at[c], sem_r.at[c])
        for d in range(DP - 1):
            total = total + rbuf[c, d].astype(jnp.float32)
        hnew[c] = total.astype(jnp.bfloat16)

        @pl.when(jnp.logical_not(last))
        def _():
            for n in range(DP):
                to_z = (z + n) % DP
                remote(
                    hnew.at[c], hbuf.at[c, row_own, col_own],
                    snd_h.at[c], sem_h.at[c], sec + GROUP, to_z,
                ).start()

        @pl.when(last)
        def _():
            for k in range(GROUP):
                to_sec = c * GROUP + k
                to_z = 2 * g + e_own
                here = (to_sec == sec) & (to_z == z)

                @pl.when(here)
                def _():
                    pltpu.make_async_copy(hnew.at[c], outb.at[:, col_own], sem_o).start()

                @pl.when(jnp.logical_not(here))
                def _():
                    remote(
                        hnew.at[c], outb.at[:, col_own], snd_h.at[c], sem_o, to_sec, to_z
                    ).start()

        return 0

    lax.fori_loop(0, CHUNKS, step, 0)

    drain(outb, sem_o)
    out_ref[...] = outb[...]

    def sent(c, _):
        drain(rbuf.at[c], snd_r.at[c])

        @pl.when(jnp.logical_not(last))
        def _():
            drain(hbuf.at[c], snd_h.at[c])

        @pl.when(last)
        def _():
            own = (c == CHUNKS - 1) & (z == 2 * g + e_own)

            @pl.when(own)
            def _():
                drain(outb.at[:, pl.ds(0, 3 * PIECE)], snd_h.at[c])

            @pl.when(jnp.logical_not(own))
            def _():
                drain(outb, snd_h.at[c])

        @pl.when(feeds)
        def _():
            drain(x_ref.at[0, pl.ds(0, LEN - CHUNK), :], snd_i.at[c])

        d = c
        drain(block(g, d), snd_y.at[d])
        drain(block(g, d), snd_c.at[d])
        drain(block(slot_y, d), snd_c2.at[d])

        @pl.when(zg == g)
        def _():
            drain(block(4, d), snd_yx.at[d])

        @pl.when((zg == g) | (zg == slot_y))
        def _():
            drain(block(4, d), snd_cx.at[d])

        @pl.when(d > 0)
        def _():
            drain(block(g, 0), sem_w.at[d])

        return 0

    lax.fori_loop(0, CHUNKS, sent, 0)
    for m in range(2):
        @pl.when(z != g + GROUP * m)
        def _():
            drain(block(g, 0), sem_w.at[DP + m])

    @pl.when(own_seq)
    def _():
        for d in range(1, DP):
            drain(ks_ref, snd_k.at[d - 1])


def shards(inputs, span_lengths, qkv_weight, out_weight):
    sections = lax.axis_size("section")
    lengths = span_lengths[0]
    ends = jnp.cumsum(lengths)
    starts = ends - lengths
    pos = jnp.arange(LEN, dtype=jnp.int32)
    seg = jnp.sum((ends[None, :] <= pos[:, None]).astype(jnp.int32), axis=1)
    prev = jnp.maximum(seg - 1, 0)
    ids = jnp.arange(SPANS, dtype=jnp.int32)
    key_start = jnp.sum(jnp.where(ids[None, :] == prev[:, None], starts[None, :], 0), axis=1)
    key_start = jnp.broadcast_to(key_start.astype(jnp.bfloat16)[:, None], (LEN, HD))

    bf16 = jnp.bfloat16
    dma = lambda *n: pltpu.SemaphoreType.DMA(n)
    out = pl.pallas_call(
        kernel,
        out_shape=jax.ShapeDtypeStruct((CHUNK, WIDTH), bf16),
        in_specs=[pl.BlockSpec(memory_space=pl.ANY)] * 4,
        out_specs=pl.BlockSpec(memory_space=pltpu.VMEM),
        scratch_shapes=[
            pltpu.VMEM((SLOTS, WIDTH, 4 * HD), bf16),
            pltpu.VMEM((CHUNKS, 2 * CHUNK, WIDTH), bf16),
            pltpu.VMEM((2 * CHUNK, WIDTH), bf16),
            pltpu.VMEM((2, LEN + BACK, SLOTS * HD), bf16),
            pltpu.VMEM((2, LEN + BACK, SLOTS * HD), bf16),
            pltpu.VMEM((2, LEN, HD), bf16),
            pltpu.VMEM((2 * CHUNK, WIDTH), jnp.float32),
            pltpu.VMEM((CHUNKS, 2 * CHUNK, WIDTH), bf16),
            pltpu.VMEM((CHUNKS, DP - 1, CHUNK, PIECE), bf16),
            pltpu.VMEM((CHUNKS, CHUNK, PIECE), bf16),
            pltpu.VMEM((CHUNK, WIDTH), bf16),
            dma(DP + 2), dma(DP), dma(DP), dma(DP), dma(DP), dma(DP), dma(DP), dma(DP),
            dma(DP), dma(DP), dma(DP), dma(DP), dma(DP),
            pltpu.SemaphoreType.DMA, dma(DP - 1), dma(CHUNKS), dma(CHUNKS), dma(CHUNKS),
            dma(CHUNKS), dma(CHUNKS), pltpu.SemaphoreType.DMA,
        ],
        compiler_params=pltpu.CompilerParams(
            has_side_effects=True, vmem_limit_bytes=44 * 1024 * 1024
        ),
    )(inputs, key_start, qkv_weight, out_weight)
    rows = LEN // sections
    first = lax.axis_index("section") % (CHUNK // rows) * rows
    return lax.dynamic_slice(out, (first, 0), (rows, WIDTH))[None]


def solution(mesh):
    in_specs = (
        P("dp", None, None),
        P("dp", None),
        P("section", "dp", None),
        P("section", "dp", None),
    )
    out_specs = P("dp", "section", None)
    return jax.shard_map(shards, mesh=mesh, in_specs=in_specs, out_specs=out_specs, check_vma=False)
```

time: 1010 us -> 377 us (0.37)
  waiting for transfers between devices: 647 us -> 0 us
  Pallas kernels: 0 us -> 370 us
  matrix products: 148 us -> 0 us
  starting transfers between devices: 70.1 us -> 0 us
  loops' own time: 62.2 us -> 0 us
  other arithmetic: 34.5 us -> 1.67 us
  local copies, waits for them, and re-layouts: 32.5 us -> 4.63 us
  between operations: 13.2 us -> 0.05 us
    pallas_call x0 -> x1, Pallas kernels: none -> 370 us  [shards(): pl.pallas_call(kernel, out_shape=jax.ShapeDtypeStruct((CHUNK, WIDTH), bf1...]
    all_gather x2 -> x0, waiting for transfers between devices: 278 us -> none  [the longest x1 200 us: shards(): lax.all_gather(qkv_weight, 'dp', axis=1, tiled=True)]
    ppermute x45 -> x0, waiting for transfers between devices: 255 us -> none  [the longest x15 189 us: from_behind(): return lax.ppermute(array, axis, pairs)]
    dot_general x39 -> x0, matrix products: 148 us -> none  [the longest x8 74.7 us: attend(): jnp.dot(normed, qkv_mat, preferred_element_type=jnp.float32)]
    psum x1 -> x0, waiting for transfers between devices: 112 us -> none  [spread(): return lax.psum(jnp.where(mine, array, jnp.zeros_like(array)), axis)]
    ppermute x45 -> x0, starting transfers between devices: 70 us -> none  [the longest x30 50.6 us: from_partner(): return lax.ppermute(block, axis, route)]
    another operation x16 -> x0, loops' own time: 62.2 us -> none  [the longest x15 32.8 us: advance(): lax.cond(active, attend, spare, h_in, key_cache, value_cache, seg_start,...]
    dynamic_update_slice x31 -> x0, local copies, waits for them, and re-layouts: 28.1 us -> none  [the longest x15 17.3 us: advance(): finished = lax.dynamic_update_slice(finished, new_slot, (seg_start, 0))]
  transfers between devices with their start and end apart: 48 -> 0, of which waited for: 48 -> 0; matrix products, arithmetic and copies ran while one was open for 2% -> 0% of each run, Pallas kernels for 0% -> 0%
where the time goes in v1:
time: 377 us
  Pallas kernels  370 us (98%)
  local copies, waits for them, and re-layouts  4.63 us (1%)
    pallas_call x1, Pallas kernels, shards(): pl.pallas_call(kernel, out_shape=jax.ShapeDtypeStruct((CHUNK, WIDTH), bf1...  370 us

profile of v1, /device:TPU:23, one launch (start us, length us, event | category | flops | bytes accessed | tf_op | source)
XLA Modules:
  0.0 376.6 jit_solution(4895319434169928312)
XLA Ops:
  0.0 0.8 reduce-window.4
  0.8 0.7 fusion
  1.5 0.1 convert_reduce_fusion
  1.6 0.1 select_reduce_fusion
  1.7 0.1 broadcast_in_dim.31.ks_ref
  1.8 0.0 copy-start
  1.8 1.7 copy-done
  3.5 0.0 copy-start.1
  3.5 1.1 copy-done.1
  4.6 0.0 copy-start.2
  4.6 1.1 copy-done.2
  5.7 370.2 %shard_map.46 = bf16[16,2560]{1,0:T(8,128)(2,1)S(1)} custom-call(bf16[1,128,2560]{2,1,0:T(8,128)(2,1)S(1)} %copy-done.2, bf16[128,128]{1,0:T(8,128)(2,1)S(1)} %broadcast_in_dim.31.ks_ref, bf16[1,320,3840]{2,1,0:T(8,128)(2,1)S(1)} %copy-done, bf16[1,320,1280]{2,1,0:T(8,128)(2,1)S(1)} %copy-done.1), custom_call_target="tpu_custom_call" | custom-call | tf_op jit(solution)/shard_map/pallas_call | solution.py:363
  375.9 0.6 dynamic-slice_bitcast_fusion
  (2 shorter events, 0.0 us)
Async XLA Ops:
  1.8 1.7 copy-start
  3.5 1.1 copy-start.1
  4.6 1.1 copy-start.2

commit v2 on v1

v2 whole, which is shorter than its diff:
```python
import jax
import jax.numpy as jnp
from jax import lax
from jax.experimental import pallas as pl
from jax.experimental.pallas import tpu as pltpu
from jax.sharding import PartitionSpec as P

HD = 128
GROUP = 4
SPANS = 8
LEN = 128
DP = 8
WIDTH = 2560
ROWS = 320
SLOTS = 5
CHUNK = 16
CHUNKS = LEN // CHUNK
BACK = 48
KEYS = BACK + CHUNK
PIECE = 640
AHEAD = 2
MESH = pl.DeviceIdType.MESH


def kernel(
    x_ref, sp_ref, qkv_ref, ow_ref, out_ref,
    w, hbuf, normed, qbuf, kc, vc, span, first_ref, part, sendb, rbuf, hnew, outb,
    sem_w, sem_z, sem_x, sem_y, sem_yx, sem_c, sem_c2, sem_cx,
    snd_y, snd_yx, snd_c, snd_c2, snd_cx, snd_cx2,
    sem_k, snd_k, sem_h, snd_i, sem_r, snd_r, snd_h, sem_o,
):
    sec = lax.axis_index("section")
    z = lax.axis_index("dp")
    sections = lax.axis_size("section")
    layers = sections // GROUP
    layer = sec // GROUP
    last = layer == layers - 1
    g = sec % GROUP
    base = layer * GROUP
    slot_y = (g + 2) % GROUP
    y_mate = base + slot_y
    mate = g + 1 - 2 * (g % 2)
    c_mate = base + mate
    slot_cy = (mate + 2) % GROUP
    zg = z % GROUP

    q = (g + 2 * (layer % 2)) % GROUP
    q_z = (z % 2) * 2 + z % GROUP // 2
    e_z = z // GROUP
    own_seq = q_z == q
    e_own = z // GROUP
    cc_own = z % GROUP
    out_z = GROUP * e_own + 2 * (q % 2) + q // 2
    is_out = out_z == z

    def remote(src, dst, s_sem, r_sem, to_sec, to_z):
        return pltpu.make_async_remote_copy(
            src_ref=src, dst_ref=dst, send_sem=s_sem, recv_sem=r_sem,
            device_id=(to_sec, to_z), device_id_type=MESH,
        )

    def drain(ref, sem):
        pltpu.make_async_copy(ref, ref, sem).wait()

    barrier = pltpu.get_barrier_semaphore()

    def greet(to_sec, to_z):
        pl.semaphore_signal(barrier, inc=1, device_id=(to_sec, to_z), device_id_type=MESH)

    for d in range(1, DP):
        greet(sec, (z + d) % DP)
    greet(y_mate, z)
    greet(c_mate, z)
    for d in range(1, DP):
        greet(y_mate, (z + d) % DP)

    @pl.when(layer > 0)
    def _():
        for d in range(DP):
            greet(base - GROUP + slot_y, (z + d) % DP)

    g_out = (q_z + 2 * ((layers - 1) % 2)) % GROUP
    for cc in range(GROUP):
        from_sec, from_z = sections - GROUP + g_out, e_z * GROUP + cc

        @pl.when((from_sec != sec) | (from_z != z))
        def _():
            greet(from_sec, from_z)

    kc[:, pl.ds(0, BACK), :] = jnp.zeros((2, BACK, SLOTS * HD), jnp.bfloat16)
    vc[:, pl.ds(0, BACK), :] = jnp.zeros((2, BACK, SLOTS * HD), jnp.bfloat16)
    span[2] = jnp.zeros((8, HD), jnp.int32)
    span[2, pl.ds(0, 1), pl.ds(0, SPANS)] = sp_ref[...]

    @pl.when(jnp.logical_not(last))
    def _():
        pl.semaphore_wait(barrier, 2 * DP + DP)

    @pl.when(last & is_out)
    def _():
        pl.semaphore_wait(barrier, 2 * DP + sections - 1)

    @pl.when(last & jnp.logical_not(is_out))
    def _():
        pl.semaphore_wait(barrier, 2 * DP + sections)

    @pl.when(own_seq)
    def _():
        pltpu.make_async_copy(span.at[2], span.at[e_z], sem_k).start()
        for d in range(1, DP):
            remote(span.at[2], span.at[e_z], snd_k.at[d - 1], sem_k, sec, (z + d) % DP).start()

    feeds = own_seq & (layer == 0)

    def feed(c):
        src = x_ref.at[0, pl.ds(pl.multiple_of(c * CHUNK, CHUNK), CHUNK), :]
        dst = hbuf.at[c, pl.ds(pl.multiple_of(e_z * CHUNK, CHUNK), CHUNK), :]
        pltpu.make_async_copy(src, dst, sem_h.at[c]).start()
        for d in range(1, DP):
            remote(src, dst, snd_i.at[c], sem_h.at[c], sec, (z + d) % DP).start()

    def parts(i, slot):
        rows = pl.ds(pl.multiple_of(z * ROWS, ROWS), ROWS)
        col = lambda n: pl.ds(pl.multiple_of(n * HD, HD), HD)
        out = []
        for p in range(3):
            out.append((qkv_ref.at[0, :, col(10 * p + i)], w.at[slot, rows, pl.ds(HD * p, HD)]))
        out.append((ow_ref.at[0, :, col(i)], w.at[slot, rows, pl.ds(3 * HD, HD)]))
        return out

    def order(n):
        return ((1 - 2 * (n % 2)) * ((n + 1) // 2) + DP) % DP

    def send_round(n):
        d = order(n)
        to_z = (z + d) % DP
        head = parts(to_z, g)

        @pl.when(to_z == z)
        def _():
            for src, dst in head:
                pltpu.make_async_copy(src, dst, sem_z.at[0]).start()

        @pl.when(to_z != z)
        def _():
            for src, dst in head:
                remote(src, dst, sem_w.at[n], sem_z.at[d], sec, to_z).start()

        @pl.when(to_z % GROUP == g)
        def _():
            m = to_z // GROUP
            extra = parts(8 + m, 4)

            @pl.when(to_z == z)
            def _():
                for src, dst in extra[:2]:
                    pltpu.make_async_copy(src, dst, sem_x.at[0]).start()

            @pl.when(to_z != z)
            def _():
                for src, dst in extra[:2]:
                    remote(src, dst, sem_w.at[DP + m], sem_x.at[d], sec, to_z).start()

            for src, dst in extra[2:]:
                remote(src, dst, sem_w.at[DP + 2 + m], sem_x.at[d], y_mate, to_z).start()

    def block(slot, d):
        return w.at[slot, pl.ds(pl.multiple_of((z + DP - d) % DP * ROWS, ROWS), ROWS), :]

    takes = (zg == g) | (zg == slot_y)
    mine = jnp.where(zg == g, 0, 2 * HD)

    def half(d, at):
        rows = pl.ds(pl.multiple_of((z + DP - d) % DP * ROWS, ROWS), ROWS)
        return w.at[4, rows, pl.ds(pl.multiple_of(at, 2 * HD), 2 * HD)]

    for n in range(AHEAD):
        send_round(n)

    @pl.when(feeds)
    def _():
        feed(0)

    def relay(n, _):
        @pl.when(n + AHEAD < DP)
        def _():
            send_round(n + AHEAD)

        @pl.when(n < DP)
        def _():
            d = order(n)
            b = block(g, d)
            drain(b, sem_z.at[d])
            remote(b, b, snd_y.at[d], sem_y.at[d], y_mate, z).start()
            remote(b, b, snd_c.at[d], sem_c.at[d], c_mate, z).start()

            @pl.when(takes)
            def _():
                x = half(d, mine)
                drain(x, sem_x.at[d])
                remote(x, x, snd_yx.at[d], sem_yx.at[d], y_mate, z).start()
                remote(x, x, snd_cx.at[d], sem_cx.at[d], c_mate, z).start()

        @pl.when(n > 0)
        def _():
            d = order(n - 1)
            b = block(slot_y, d)
            drain(b, sem_y.at[d])
            remote(b, b, snd_c2.at[d], sem_c2.at[d], c_mate, z).start()

            @pl.when(takes)
            def _():
                x = half(d, 2 * HD - mine)
                drain(x, sem_yx.at[d])
                remote(x, x, snd_cx2.at[d], sem_cx.at[d], c_mate, z).start()

        return 0

    lax.fori_loop(0, DP + 1, relay, 0)

    drain(span.at[pl.ds(0, 2)], sem_k)
    lane = lax.broadcasted_iota(jnp.int32, (1, HD), 1)
    token = lax.broadcasted_iota(jnp.int32, (LEN, HD), 0).astype(jnp.float32)
    for e in range(2):
        lens = span[e, pl.ds(0, 1), :].astype(jnp.float32)
        key_start = jnp.zeros((LEN, HD), jnp.float32)
        before = jnp.zeros((1, 1), jnp.float32)
        for s in range(1, SPANS):
            start = jnp.sum(jnp.where(lane < s, lens, 0.0), axis=1, keepdims=True)
            key_start = jnp.where(token >= start, before, key_start)
            before = start
        first_ref[e] = key_start

    def arrive(n, _):
        d = order(n)
        drain(block(mate, d), sem_c.at[d])
        drain(block(slot_cy, d), sem_c2.at[d])

        @pl.when(jnp.logical_not(takes))
        def _():
            drain(block(4, d), sem_cx.at[d])

        return 0

    lax.fori_loop(0, DP, arrive, 0)

    row_own = pl.ds(pl.multiple_of(e_own * CHUNK, CHUNK), CHUNK)
    col_own = pl.ds(pl.multiple_of(cc_own * PIECE, PIECE), PIECE)
    scale = HD ** (-0.5)

    def project(c):
        drain(hbuf.at[c], sem_h.at[c])
        values = hbuf[c].astype(jnp.float32)
        mean = jnp.mean(values, axis=-1, keepdims=True)
        centred = values - mean
        var = jnp.mean(centred * centred, axis=-1, keepdims=True)
        normed[...] = (centred * lax.rsqrt(var + 1e-05)).astype(jnp.bfloat16)

        def columns(cols):
            mat = [w[s, :, pl.ds(p * HD, HD * n)] for s, p, n in cols]
            mat = mat[0] if len(mat) == 1 else jnp.concatenate(mat, axis=1)
            return jnp.dot(normed[...], mat, preferred_element_type=jnp.float32).astype(jnp.bfloat16)

        new = pl.ds(pl.multiple_of(c * CHUNK + BACK, CHUNK), CHUNK)
        for s in range(SLOTS):
            qk = columns([(s, 0, 2)])
            qbuf[s] = qk[:, :HD]
            kc[0, new, pl.ds(s * HD, HD)] = qk[:CHUNK, HD:]
            kc[1, new, pl.ds(s * HD, HD)] = qk[CHUNK:, HD:]
        for s in (0, 2, 4):
            n = 2 if s < 4 else 1
            v = columns([(s + i, 2, 1) for i in range(n)])
            vc[0, new, pl.ds(s * HD, n * HD)] = v[:CHUNK]
            vc[1, new, pl.ds(s * HD, n * HD)] = v[CHUNK:]

    def attend(c):
        tok = pl.ds(pl.multiple_of(c * CHUNK, CHUNK), CHUNK)
        first = jnp.concatenate([first_ref[0, tok, :], first_ref[1, tok, :]], axis=0)
        row = lax.broadcasted_iota(jnp.int32, (2 * CHUNK, 2 * KEYS), 0)
        col = lax.broadcasted_iota(jnp.int32, (2 * CHUNK, 2 * KEYS), 1)
        same = (row < CHUNK) == (col < KEYS)
        key_pos = c * CHUNK - BACK + jnp.where(col < KEYS, col, col - KEYS)
        tok_pos = c * CHUNK + jnp.where(row < CHUNK, row, row - CHUNK)
        allowed = same & (key_pos <= tok_pos) & (key_pos.astype(jnp.float32) >= first)

        window = pl.ds(pl.multiple_of(c * CHUNK, CHUNK), KEYS)
        attended = []
        for s in range(SLOTS):
            cols = pl.ds(s * HD, HD)
            keys = jnp.concatenate([kc[0, window, cols], kc[1, window, cols]], axis=0)
            vals = jnp.concatenate([vc[0, window, cols], vc[1, window, cols]], axis=0)
            scores = lax.dot_general(
                qbuf[s], keys, (((1,), (1,)), ((), ())), preferred_element_type=jnp.float32
            ) * scale
            weights = jnp.where(allowed, jnp.exp(scores), 0.0)
            probs = (weights / jnp.sum(weights, axis=-1, keepdims=True)).astype(jnp.bfloat16)
            attended.append(
                jnp.dot(probs, vals, preferred_element_type=jnp.float32).astype(jnp.bfloat16)
            )

        for cc in range(GROUP):
            total = None
            rows = pl.ds(cc * PIECE, PIECE)
            for s in (0, 2, 4):
                n = 2 if s < 4 else 1
                lhs = attended[s] if n == 1 else jnp.concatenate(attended[s : s + n], axis=1)
                rhs = [w[s + i, rows, pl.ds(3 * HD, HD)] for i in range(n)]
                rhs = rhs[0] if n == 1 else jnp.concatenate(rhs, axis=1)
                term = lax.dot_general(
                    lhs, rhs, (((1,), (1,)), ((), ())), preferred_element_type=jnp.float32
                )
                total = term if total is None else total + term
            cols = pl.ds(cc * PIECE, PIECE)
            part[:, cols] = total
            sendb[c, :, cols] = total.astype(jnp.bfloat16)
            for e in range(2):
                to_z = e * GROUP + cc

                @pl.when(z != to_z)
                def _():
                    d = (to_z - z + DP) % DP
                    remote(
                        sendb.at[c, pl.ds(e * CHUNK, CHUNK), cols], rbuf.at[c, d - 1],
                        snd_r.at[c], sem_r.at[c], sec, to_z,
                    ).start()

    def combine(c):
        total = part[row_own, col_own] + hbuf[c, row_own, col_own].astype(jnp.float32)
        drain(rbuf.at[c], sem_r.at[c])
        for d in range(DP - 1):
            total = total + rbuf[c, d].astype(jnp.float32)
        hnew[c] = total.astype(jnp.bfloat16)

        @pl.when(jnp.logical_not(last))
        def _():
            for n in range(DP):
                remote(
                    hnew.at[c], hbuf.at[c, row_own, col_own],
                    snd_h.at[c], sem_h.at[c], base + GROUP + slot_y, (z + n) % DP,
                ).start()

        @pl.when(last)
        def _():
            for k in range(GROUP):
                to_sec = c * GROUP + k
                here = (to_sec == sec) & is_out

                @pl.when(here)
                def _():
                    pltpu.make_async_copy(hnew.at[c], outb.at[:, col_own], sem_o).start()

                @pl.when(jnp.logical_not(here))
                def _():
                    remote(
                        hnew.at[c], outb.at[:, col_own], snd_h.at[c], sem_o, to_sec, out_z
                    ).start()

    def step(c, _):
        @pl.when(feeds & (c < CHUNKS - 1))
        def _():
            feed(c + 1)

        project(c)
        attend(c)
        combine(c)
        return 0

    lax.fori_loop(0, CHUNKS, step, 0)

    drain(outb, sem_o)
    out_ref[...] = outb[...]

    def sent(c, _):
        drain(rbuf.at[c], snd_r.at[c])

        @pl.when(jnp.logical_not(last))
        def _():
            drain(hbuf.at[c], snd_h.at[c])

        @pl.when(last)
        def _():
            own = (c == CHUNKS - 1) & is_out

            @pl.when(own)
            def _():
                drain(outb.at[:, pl.ds(0, 3 * PIECE)], snd_h.at[c])

            @pl.when(jnp.logical_not(own))
            def _():
                drain(outb, snd_h.at[c])

        @pl.when(feeds)
        def _():
            drain(x_ref.at[0, pl.ds(0, LEN - CHUNK), :], snd_i.at[c])

        d = c
        drain(block(g, d), snd_y.at[d])
        drain(block(g, d), snd_c.at[d])
        drain(block(slot_y, d), snd_c2.at[d])

        @pl.when(takes)
        def _():
            drain(half(d, mine), snd_yx.at[d])
            drain(half(d, mine), snd_cx.at[d])
            drain(half(d, mine), snd_cx2.at[d])

        @pl.when(d > 0)
        def _():
            drain(block(g, 0), sem_w.at[d])

        return 0

    lax.fori_loop(0, CHUNKS, sent, 0)
    for m in range(2):
        @pl.when(z != g + GROUP * m)
        def _():
            drain(half(0, 0), sem_w.at[DP + m])

        drain(half(0, 0), sem_w.at[DP + 2 + m])

    @pl.when(own_seq)
    def _():
        for d in range(1, DP):
            drain(span.at[2], snd_k.at[d - 1])


def shards(inputs, span_lengths, qkv_weight, out_weight):
    sections = lax.axis_size("section")
    bf16 = jnp.bfloat16
    dma = lambda *n: pltpu.SemaphoreType.DMA(n)
    out = pl.pallas_call(
        kernel,
        out_shape=jax.ShapeDtypeStruct((CHUNK, WIDTH), bf16),
        in_specs=[
            pl.BlockSpec(memory_space=pl.ANY),
            pl.BlockSpec(memory_space=pltpu.VMEM),
            pl.BlockSpec(memory_space=pl.ANY),
            pl.BlockSpec(memory_space=pl.ANY),
        ],
        out_specs=pl.BlockSpec(memory_space=pltpu.VMEM),
        scratch_shapes=[
            pltpu.VMEM((SLOTS, WIDTH, 4 * HD), bf16),
            pltpu.VMEM((CHUNKS, 2 * CHUNK, WIDTH), bf16),
            pltpu.VMEM((2 * CHUNK, WIDTH), bf16),
            pltpu.VMEM((SLOTS, 2 * CHUNK, HD), bf16),
            pltpu.VMEM((2, LEN + BACK, SLOTS * HD), bf16),
            pltpu.VMEM((2, LEN + BACK, SLOTS * HD), bf16),
            pltpu.VMEM((3, 8, HD), jnp.int32),
            pltpu.VMEM((2, LEN, HD), jnp.float32),
            pltpu.VMEM((2 * CHUNK, WIDTH), jnp.float32),
            pltpu.VMEM((CHUNKS, 2 * CHUNK, WIDTH), bf16),
            pltpu.VMEM((CHUNKS, DP - 1, CHUNK, PIECE), bf16),
            pltpu.VMEM((CHUNKS, CHUNK, PIECE), bf16),
            pltpu.VMEM((CHUNK, WIDTH), bf16),
            dma(DP + 4), dma(DP), dma(DP), dma(DP), dma(DP), dma(DP), dma(DP), dma(DP),
            dma(DP), dma(DP), dma(DP), dma(DP), dma(DP), dma(DP),
            pltpu.SemaphoreType.DMA, dma(DP - 1), dma(CHUNKS), dma(CHUNKS), dma(CHUNKS),
            dma(CHUNKS), dma(CHUNKS), pltpu.SemaphoreType.DMA,
        ],
        compiler_params=pltpu.CompilerParams(
            collective_id=0, has_side_effects=True, vmem_limit_bytes=60 * 1024 * 1024
        ),
    )(inputs, span_lengths, qkv_weight, out_weight)
    rows = LEN // sections
    first = lax.axis_index("section") % (CHUNK // rows) * rows
    return lax.dynamic_slice(out, (first, 0), (rows, WIDTH))[None]


def solution(mesh):
    in_specs = (
        P("dp", None, None),
        P("dp", None),
        P("section", "dp", None),
        P("section", "dp", None),
    )
    out_specs = P("dp", "section", None)
    return jax.shard_map(shards, mesh=mesh, in_specs=in_specs, out_specs=out_specs, check_vma=False)
```

time: 377 us -> 346 us (0.918)
  Pallas kernels: 370 us -> 342 us
    pallas_call x1, Pallas kernels: 370 us -> 342 us  [shards(): pl.pallas_call(kernel, out_shape=jax.ShapeDtypeStruct((CHUNK, WIDTH), bf1...]
    unnamed x6 -> x0, local copies, waits for them, and re-layouts: 3.92 us -> none
where the time goes in v2:
time: 346 us; the launch traced here: 343 us
  Pallas kernels  342 us (99%)
    pallas_call x1, Pallas kernels, shards(): pl.pallas_call(kernel, out_shape=jax.ShapeDtypeStruct((CHUNK, WIDTH), bf1...  342 us

profile of v2, /device:TPU:23, one launch (start us, length us, event | category | flops | bytes accessed | tf_op | source)
XLA Modules:
  0.0 343.0 jit_solution(2394228155149797887)
XLA Ops:
  0.0 341.6 %shard_map.46 = bf16[16,2560]{1,0:T(8,128)(2,1)} custom-call(bf16[1,128,2560]{2,1,0:T(8,128)(2,1)} %x_ref.1, s32[1,8]{1,0:T(1,128)} %sp_ref.1, bf16[1,320,3840]{2,1,0:T(8,128)(2,1)} %qkv_ref.1, bf16[1,320,1280]{2,1,0:T(8,128)(2,1)} %ow_ref.1), custom_call_target="tpu_custom_call" | custom-call | tf_op jit(solution)/shard_map/pallas_call | solution.py:431
  341.6 1.4 dynamic-slice_bitcast_fusion

commit v3 on v2

--- a/solution.py
+++ b/solution.py
@@ -19,6 +19,7 @@
 KEYS = BACK + CHUNK
 PIECE = 640
 AHEAD = 2
+FAR = (0, 3, 1, 2)
 MESH = pl.DeviceIdType.MESH
 
 
@@ -27,7 +28,7 @@
     w, hbuf, normed, qbuf, kc, vc, span, first_ref, part, sendb, rbuf, hnew, outb,
     sem_w, sem_z, sem_x, sem_y, sem_yx, sem_c, sem_c2, sem_cx,
     snd_y, snd_yx, snd_c, snd_c2, snd_cx, snd_cx2,
-    sem_k, snd_k, sem_h, snd_i, sem_r, snd_r, snd_h, sem_o,
+    sem_k, snd_k, sem_h, snd_i, sem_r, snd_r, snd_h, sem_o, sem_f, snd_f,
 ):
     sec = lax.axis_index("section")
     z = lax.axis_index("dp")
@@ -48,10 +49,11 @@
     q_z = (z % 2) * 2 + z % GROUP // 2
     e_z = z // GROUP
     own_seq = q_z == q
+    feeds = (layer >= layers // 2) & (q_z == g)
     e_own = z // GROUP
     cc_own = z % GROUP
     out_z = GROUP * e_own + 2 * (q % 2) + q // 2
-    is_out = out_z == z
+    is_out = (out_z == z) & (cc_own == g)
 
     def remote(src, dst, s_sem, r_sem, to_sec, to_z):
         return pltpu.make_async_remote_copy(
@@ -79,30 +81,27 @@
         for d in range(DP):
             greet(base - GROUP + slot_y, (z + d) % DP)
 
+    @pl.when(layer == 0)
+    def _():
+        for n in range(layers // 2):
+            for e in range(2):
+                greet((layers // 2 + n) * GROUP + g, 4 * e + 2 * (g % 2) + g // 2)
+
     g_out = (q_z + 2 * ((layers - 1) % 2)) % GROUP
-    for cc in range(GROUP):
-        from_sec, from_z = sections - GROUP + g_out, e_z * GROUP + cc
-
-        @pl.when((from_sec != sec) | (from_z != z))
-        def _():
-            greet(from_sec, from_z)
+    from_sec, from_z = sections - GROUP + g_out, e_z * GROUP + g
+    greet(base + GROUP - 1 - g, z)
+
+    @pl.when((from_sec != sec) | (from_z != z))
+    def _():
+        greet(from_sec, from_z)
 
     kc[:, pl.ds(0, BACK), :] = jnp.zeros((2, BACK, SLOTS * HD), jnp.bfloat16)
     vc[:, pl.ds(0, BACK), :] = jnp.zeros((2, BACK, SLOTS * HD), jnp.bfloat16)
     span[2] = jnp.zeros((8, HD), jnp.int32)
     span[2, pl.ds(0, 1), pl.ds(0, SPANS)] = sp_ref[...]
 
-    @pl.when(jnp.logical_not(last))
-    def _():
-        pl.semaphore_wait(barrier, 2 * DP + DP)
-
-    @pl.when(last & is_out)
-    def _():
-        pl.semaphore_wait(barrier, 2 * DP + sections - 1)
-
-    @pl.when(last & jnp.logical_not(is_out))
-    def _():
-        pl.semaphore_wait(barrier, 2 * DP + sections)
+    partners = 2 * DP + 1 + jnp.where(last, layers - is_out.astype(jnp.int32), DP)
+    pl.semaphore_wait(barrier, partners + DP * feeds.astype(jnp.int32))
 
     @pl.when(own_seq)
     def _():
@@ -110,14 +109,16 @@
         for d in range(1, DP):
             remote(span.at[2], span.at[e_z], snd_k.at[d - 1], sem_k, sec, (z + d) % DP).start()
 
-    feeds = own_seq & (layer == 0)
-
     def feed(c):
         src = x_ref.at[0, pl.ds(pl.multiple_of(c * CHUNK, CHUNK), CHUNK), :]
         dst = hbuf.at[c, pl.ds(pl.multiple_of(e_z * CHUNK, CHUNK), CHUNK), :]
-        pltpu.make_async_copy(src, dst, sem_h.at[c]).start()
-        for d in range(1, DP):
-            remote(src, dst, snd_i.at[c], sem_h.at[c], sec, (z + d) % DP).start()
+        for d in range(DP):
+            remote(src, dst, snd_i.at[c % 2], sem_h.at[c], g, (z + d) % DP).start()
+
+    @pl.when(feeds)
+    def _():
+        for n in range(2):
+            feed(2 * (layer - layers // 2) + n)
 
     def parts(i, slot):
         rows = pl.ds(pl.multiple_of(z * ROWS, ROWS), ROWS)
@@ -176,10 +177,6 @@
 
     for n in range(AHEAD):
         send_round(n)
-
-    @pl.when(feeds)
-    def _():
-        feed(0)
 
     def relay(n, _):
         @pl.when(n + AHEAD < DP)
@@ -298,9 +295,10 @@
                 jnp.dot(probs, vals, preferred_element_type=jnp.float32).astype(jnp.bfloat16)
             )
 
-        for cc in range(GROUP):
+        for turn in range(GROUP):
+            cc = (cc_own + FAR[turn]) % GROUP
             total = None
-            rows = pl.ds(cc * PIECE, PIECE)
+            rows = pl.ds(pl.multiple_of(cc * PIECE, PIECE), PIECE)
             for s in (0, 2, 4):
                 n = 2 if s < 4 else 1
                 lhs = attended[s] if n == 1 else jnp.concatenate(attended[s : s + n], axis=1)
@@ -310,17 +308,15 @@
                     lhs, rhs, (((1,), (1,)), ((), ())), preferred_element_type=jnp.float32
                 )
                 total = term if total is None else total + term
-            cols = pl.ds(cc * PIECE, PIECE)
+            cols = pl.ds(pl.multiple_of(cc * PIECE, PIECE), PIECE)
             part[:, cols] = total
             sendb[c, :, cols] = total.astype(jnp.bfloat16)
-            for e in range(2):
-                to_z = e * GROUP + cc
-
-                @pl.when(z != to_z)
-                def _():
-                    d = (to_z - z + DP) % DP
+            for d in ((FAR[turn] + GROUP), FAR[turn]):
+                if d > 0:
+                    to_z = (z + d) % DP
+                    rows = pl.ds(pl.multiple_of(to_z // GROUP * CHUNK, CHUNK), CHUNK)
                     remote(
-                        sendb.at[c, pl.ds(e * CHUNK, CHUNK), cols], rbuf.at[c, d - 1],
+                        sendb.at[c, rows, cols], rbuf.at[c, d - 1],
                         snd_r.at[c], sem_r.at[c], sec, to_z,
                     ).start()
 
@@ -333,7 +329,7 @@
 
         @pl.when(jnp.logical_not(last))
         def _():
-            for n in range(DP):
+            for n in (4, 3, 5, 2, 6, 1, 7, 0):
                 remote(
                     hnew.at[c], hbuf.at[c, row_own, col_own],
                     snd_h.at[c], sem_h.at[c], base + GROUP + slot_y, (z + n) % DP,
@@ -341,25 +337,18 @@
 
         @pl.when(last)
         def _():
-            for k in range(GROUP):
-                to_sec = c * GROUP + k
-                here = (to_sec == sec) & is_out
-
-                @pl.when(here)
-                def _():
-                    pltpu.make_async_copy(hnew.at[c], outb.at[:, col_own], sem_o).start()
-
-                @pl.when(jnp.logical_not(here))
-                def _():
-                    remote(
-                        hnew.at[c], outb.at[:, col_own], snd_h.at[c], sem_o, to_sec, out_z
-                    ).start()
+            to_sec = c * GROUP + cc_own
+            here = (to_sec == sec) & is_out
+
+            @pl.when(here)
+            def _():
+                pltpu.make_async_copy(hnew.at[c], outb.at[:, col_own], sem_o).start()
+
+            @pl.when(jnp.logical_not(here))
+            def _():
+                remote(hnew.at[c], outb.at[:, col_own], snd_h.at[c], sem_o, to_sec, out_z).start()
 
     def step(c, _):
-        @pl.when(feeds & (c < CHUNKS - 1))
-        def _():
-            feed(c + 1)
-
         project(c)
         attend(c)
         combine(c)
@@ -367,8 +356,13 @@
 
     lax.fori_loop(0, CHUNKS, step, 0)
 
-    drain(outb, sem_o)
+    result = outb.at[:, pl.ds(pl.multiple_of(g * PIECE, PIECE), PIECE)]
+    drain(result, sem_o)
+    for to_sec in (c_mate, y_mate, base + GROUP - 1 - g):
+        remote(result, result, snd_f, sem_f, to_sec, z).start()
+    drain(outb.at[:, pl.ds(0, 3 * PIECE)], sem_f)
     out_ref[...] = outb[...]
+    drain(outb.at[:, pl.ds(0, 3 * PIECE)], snd_f)
 
     def sent(c, _):
         drain(rbuf.at[c], snd_r.at[c])
@@ -379,19 +373,9 @@
 
         @pl.when(last)
         def _():
-            own = (c == CHUNKS - 1) & is_out
-
-            @pl.when(own)
-            def _():
-                drain(outb.at[:, pl.ds(0, 3 * PIECE)], snd_h.at[c])
-
-            @pl.when(jnp.logical_not(own))
-            def _():
-                drain(outb, snd_h.at[c])
-
-        @pl.when(feeds)
-        def _():
-            drain(x_ref.at[0, pl.ds(0, LEN - CHUNK), :], snd_i.at[c])
+            @pl.when((c != layer) | jnp.logical_not(is_out))
+            def _():
+                drain(hnew.at[c], snd_h.at[c])
 
         d = c
         drain(block(g, d), snd_y.at[d])
@@ -417,6 +401,11 @@
             drain(half(0, 0), sem_w.at[DP + m])
 
         drain(half(0, 0), sem_w.at[DP + 2 + m])
+
+    @pl.when(feeds)
+    def _():
+        for n in range(2):
+            drain(x_ref.at[0], snd_i.at[n])
 
     @pl.when(own_seq)
     def _():
@@ -455,7 +444,8 @@
             dma(DP + 4), dma(DP), dma(DP), dma(DP), dma(DP), dma(DP), dma(DP), dma(DP),
             dma(DP), dma(DP), dma(DP), dma(DP), dma(DP), dma(DP),
             pltpu.SemaphoreType.DMA, dma(DP - 1), dma(CHUNKS), dma(CHUNKS), dma(CHUNKS),
-            dma(CHUNKS), dma(CHUNKS), pltpu.SemaphoreType.DMA,
+            dma(CHUNKS), dma(CHUNKS), pltpu.SemaphoreType.DMA, pltpu.SemaphoreType.DMA,
+            pltpu.SemaphoreType.DMA,
         ],
         compiler_params=pltpu.CompilerParams(
             collective_id=0, has_side_effects=True, vmem_limit_bytes=60 * 1024 * 1024

time: 346 us -> 315 us (0.910)
  Pallas kernels: 342 us -> 313 us
    pallas_call x1, Pallas kernels: 342 us -> 313 us  [shards(): pl.pallas_call(kernel, out_shape=jax.ShapeDtypeStruct((CHUNK, WIDTH), bf1...]
where the time goes in v3:
time: 315 us; the launch traced here: 314 us
  Pallas kernels  313 us (99%)
    pallas_call x1, Pallas kernels, shards(): pl.pallas_call(kernel, out_shape=jax.ShapeDtypeStruct((CHUNK, WIDTH), bf1...  313 us

profile of v3, /device:TPU:23, one launch (start us, length us, event | category | flops | bytes accessed | tf_op | source)
XLA Modules:
  0.0 314.4 jit_solution(8514548572798300605)
XLA Ops:
  0.0 313.0 %shard_map.46 = bf16[16,2560]{1,0:T(8,128)(2,1)} custom-call(bf16[1,128,2560]{2,1,0:T(8,128)(2,1)} %x_ref.1, s32[1,8]{1,0:T(1,128)} %sp_ref.1, bf16[1,320,3840]{2,1,0:T(8,128)(2,1)} %qkv_ref.1, bf16[1,320,1280]{2,1,0:T(8,128)(2,1)} %ow_ref.1), custom_call_target="tpu_custom_call" | custom-call | tf_op jit(solution)/shard_map/pallas_call | solution.py:420
  313.0 1.4 dynamic-slice_bitcast_fusion

commit v4 on v3

--- a/solution.py
+++ b/solution.py
@@ -20,12 +20,15 @@
 PIECE = 640
 AHEAD = 2
 FAR = (0, 3, 1, 2)
+EARLY = 2
+GUEST = 112
 MESH = pl.DeviceIdType.MESH
 
 
 def kernel(
     x_ref, sp_ref, qkv_ref, ow_ref, out_ref,
     w, hbuf, normed, qbuf, kc, vc, span, first_ref, part, sendb, rbuf, hnew, outb,
+    staged, sem_s, snd_s, snd_g, sem_gz, sem_gc, snd_gc,
     sem_w, sem_z, sem_x, sem_y, sem_yx, sem_c, sem_c2, sem_cx,
     snd_y, snd_yx, snd_c, snd_c2, snd_cx, snd_cx2,
     sem_k, snd_k, sem_h, snd_i, sem_r, snd_r, snd_h, sem_o, sem_f, snd_f,
@@ -55,6 +58,10 @@
     out_z = GROUP * e_own + 2 * (q % 2) + q // 2
     is_out = (out_z == z) & (cc_own == g)
 
+    early = layer < EARLY
+    helps = layer >= layers - EARLY
+    shift = (layers - EARLY) * GROUP
+
     def remote(src, dst, s_sem, r_sem, to_sec, to_z):
         return pltpu.make_async_remote_copy(
             src_ref=src, dst_ref=dst, send_sem=s_sem, recv_sem=r_sem,
@@ -81,6 +88,16 @@
         for d in range(DP):
             greet(base - GROUP + slot_y, (z + d) % DP)
 
+    @pl.when(early)
+    def _():
+        for d in range(DP):
+            greet(sec + shift, (z + d) % DP)
+
+    @pl.when(helps)
+    def _():
+        greet(sec - shift, z)
+        greet(y_mate - shift, z)
+
     @pl.when(layer == 0)
     def _():
         for n in range(layers // 2):
@@ -101,7 +118,8 @@
     span[2, pl.ds(0, 1), pl.ds(0, SPANS)] = sp_ref[...]
 
     partners = 2 * DP + 1 + jnp.where(last, layers - is_out.astype(jnp.int32), DP)
-    pl.semaphore_wait(barrier, partners + DP * feeds.astype(jnp.int32))
+    partners += DP * feeds.astype(jnp.int32) + 2 * early.astype(jnp.int32)
+    pl.semaphore_wait(barrier, partners + DP * helps.astype(jnp.int32))
 
     @pl.when(own_seq)
     def _():
@@ -120,100 +138,194 @@
         for n in range(2):
             feed(2 * (layer - layers // 2) + n)
 
-    def parts(i, slot):
-        rows = pl.ds(pl.multiple_of(z * ROWS, ROWS), ROWS)
-        col = lambda n: pl.ds(pl.multiple_of(n * HD, HD), HD)
-        out = []
-        for p in range(3):
-            out.append((qkv_ref.at[0, :, col(10 * p + i)], w.at[slot, rows, pl.ds(HD * p, HD)]))
-        out.append((ow_ref.at[0, :, col(i)], w.at[slot, rows, pl.ds(3 * HD, HD)]))
-        return out
+    def hand_over():
+        rows = pl.ds(ROWS - GUEST, GUEST)
+        for r in range(4):
+            cols = pl.ds(10 * HD * r, 10 * HD)
+            src = qkv_ref.at[0, rows, cols] if r < 3 else ow_ref.at[0, rows, :]
+            for n, to_sec in enumerate((sec, y_mate)):
+                remote(
+                    src, staged.at[n, r], snd_s.at[n, r], sem_s.at[n, r], to_sec + shift, z
+                ).start()
+
+    def pass_on(r, _):
+        rows = pl.ds(pl.multiple_of(z * ROWS + ROWS - GUEST, 16), GUEST)
+        cols = pl.ds(pl.multiple_of(r * HD, HD), HD)
+        for n, slot in enumerate((g, slot_y)):
+            drain(staged.at[n, r], sem_s.at[n, r])
+            for j in (4, 3, 5, 2, 6, 1, 7, 0):
+                to_z = (z + j) % DP
+                src = staged.at[n, r, :, pl.ds(pl.multiple_of(to_z * HD, HD), HD)]
+                remote(
+                    src, w.at[slot, rows, cols], snd_g.at[n, r], sem_gz.at[z], sec - shift, to_z
+                ).start()
+            for m in range(2):
+                src = staged.at[n, r, :, pl.ds((DP + m) * HD, HD)]
+                remote(
+                    src, w.at[4, rows, cols], snd_g.at[n, r], sem_gz.at[z],
+                    sec - shift, slot + GROUP * m,
+                ).start()
+        return 0
+
+    def take_guests(n, _):
+        z_s = (z + DP - order(n)) % DP
+        rows = pl.ds(pl.multiple_of(z_s * ROWS + ROWS - GUEST, 16), GUEST)
+
+        @pl.when(takes)
+        def _():
+            drain(w.at[0, pl.ds(0, 3 * GUEST), :], sem_gz.at[z_s])
+            x = w.at[4, rows, :]
+            remote(x, x, snd_gc.at[z_s], sem_gc.at[z_s], c_mate, z).start()
+
+        @pl.when(jnp.logical_not(takes))
+        def _():
+            drain(w.at[0, pl.ds(0, 2 * GUEST), :], sem_gz.at[z_s])
+
+        for slot in (g, slot_y):
+            x = w.at[slot, rows, :]
+            remote(x, x, snd_gc.at[z_s], sem_gc.at[z_s], c_mate, z).start()
+        return 0
+
+    def settle_guests(z_s, _):
+        @pl.when(takes)
+        def _():
+            drain(w.at[0, pl.ds(0, 2 * GUEST), :], sem_gc.at[z_s])
+            drain(w.at[0, pl.ds(0, 3 * GUEST), :], snd_gc.at[z_s])
+
+        @pl.when(jnp.logical_not(takes))
+        def _():
+            drain(w.at[0, pl.ds(0, 3 * GUEST), :], sem_gc.at[z_s])
+            drain(w.at[0, pl.ds(0, 2 * GUEST), :], snd_gc.at[z_s])
+
+        return 0
+
+    takes = (zg == g) | (zg == slot_y)
+    mine = jnp.where(zg == g, 0, 2 * HD)
 
     def order(n):
         return ((1 - 2 * (n % 2)) * ((n + 1) // 2) + DP) % DP
 
-    def send_round(n):
-        d = order(n)
-        to_z = (z + d) % DP
-        head = parts(to_z, g)
-
-        @pl.when(to_z == z)
-        def _():
-            for src, dst in head:
-                pltpu.make_async_copy(src, dst, sem_z.at[0]).start()
-
-        @pl.when(to_z != z)
-        def _():
-            for src, dst in head:
-                remote(src, dst, sem_w.at[n], sem_z.at[d], sec, to_z).start()
-
-        @pl.when(to_z % GROUP == g)
-        def _():
-            m = to_z // GROUP
-            extra = parts(8 + m, 4)
+    def block(slot, d, size):
+        return w.at[slot, pl.ds(pl.multiple_of((z + DP - d) % DP * ROWS, ROWS), size), :]
+
+    def half(d, at, size):
+        rows = pl.ds(pl.multiple_of((z + DP - d) % DP * ROWS, ROWS), size)
+        return w.at[4, rows, pl.ds(pl.multiple_of(at, 2 * HD), 2 * HD)]
+
+    def relayout(size):
+        def parts(i, slot):
+            rows = pl.ds(pl.multiple_of(z * ROWS, ROWS), size)
+            col = lambda n: pl.ds(pl.multiple_of(n * HD, HD), HD)
+            out = []
+            for p in range(3):
+                out.append((qkv_ref.at[0, pl.ds(0, size), col(10 * p + i)], w.at[slot, rows, pl.ds(HD * p, HD)]))
+            out.append((ow_ref.at[0, pl.ds(0, size), col(i)], w.at[slot, rows, pl.ds(3 * HD, HD)]))
+            return out
+
+        def send_round(n):
+            d = order(n)
+            to_z = (z + d) % DP
+            head = parts(to_z, g)
 
             @pl.when(to_z == z)
             def _():
-                for src, dst in extra[:2]:
-                    pltpu.make_async_copy(src, dst, sem_x.at[0]).start()
+                for src, dst in head:
+                    pltpu.make_async_copy(src, dst, sem_z.at[0]).start()
 
             @pl.when(to_z != z)
             def _():
-                for src, dst in extra[:2]:
-                    remote(src, dst, sem_w.at[DP + m], sem_x.at[d], sec, to_z).start()
-
-            for src, dst in extra[2:]:
-                remote(src, dst, sem_w.at[DP + 2 + m], sem_x.at[d], y_mate, to_z).start()
-
-    def block(slot, d):
-        return w.at[slot, pl.ds(pl.multiple_of((z + DP - d) % DP * ROWS, ROWS), ROWS), :]
-
-    takes = (zg == g) | (zg == slot_y)
-    mine = jnp.where(zg == g, 0, 2 * HD)
-
-    def half(d, at):
-        rows = pl.ds(pl.multiple_of((z + DP - d) % DP * ROWS, ROWS), ROWS)
-        return w.at[4, rows, pl.ds(pl.multiple_of(at, 2 * HD), 2 * HD)]
-
-    for n in range(AHEAD):
-        send_round(n)
-
-    def relay(n, _):
-        @pl.when(n + AHEAD < DP)
-        def _():
-            send_round(n + AHEAD)
-
-        @pl.when(n < DP)
-        def _():
+                for src, dst in head:
+                    remote(src, dst, sem_w.at[n], sem_z.at[d], sec, to_z).start()
+
+            @pl.when(to_z % GROUP == g)
+            def _():
+                m = to_z // GROUP
+                extra = parts(8 + m, 4)
+
+                @pl.when(to_z == z)
+                def _():
+                    for src, dst in extra[:2]:
+                        pltpu.make_async_copy(src, dst, sem_x.at[0]).start()
+
+                @pl.when(to_z != z)
+                def _():
+                    for src, dst in extra[:2]:
+                        remote(src, dst, sem_w.at[DP + m], sem_x.at[d], sec, to_z).start()
+
+                for src, dst in extra[2:]:
+                    remote(src, dst, sem_w.at[DP + 2 + m], sem_x.at[d], y_mate, to_z).start()
+
+        if size < ROWS:
+            hand_over()
+        for n in range(AHEAD):
+            send_round(n)
+
+        def relay(n, _):
+            @pl.when(n + AHEAD < DP)
+            def _():
+                send_round(n + AHEAD)
+
+            @pl.when(n < DP)
+            def _():
+                d = order(n)
+                b = block(g, d, size)
+                drain(b, sem_z.at[d])
+                remote(b, b, snd_y.at[d], sem_y.at[d], y_mate, z).start()
+                remote(b, b, snd_c.at[d], sem_c.at[d], c_mate, z).start()
+
+                @pl.when(takes)
+                def _():
+                    x = half(d, mine, size)
+                    drain(x, sem_x.at[d])
+                    remote(x, x, snd_yx.at[d], sem_yx.at[d], y_mate, z).start()
+                    remote(x, x, snd_cx.at[d], sem_cx.at[d], c_mate, z).start()
+
+            @pl.when(n > 0)
+            def _():
+                d = order(n - 1)
+                b = block(slot_y, d, size)
+                drain(b, sem_y.at[d])
+                remote(b, b, snd_c2.at[d], sem_c2.at[d], c_mate, z).start()
+
+                @pl.when(takes)
+                def _():
+                    x = half(d, 2 * HD - mine, size)
+                    drain(x, sem_yx.at[d])
+                    remote(x, x, snd_cx2.at[d], sem_cx.at[d], c_mate, z).start()
+
+            return 0
+
+        lax.fori_loop(0, DP + 1, relay, 0)
+        if size < ROWS:
+            lax.fori_loop(0, DP, take_guests, 0)
+
+        def arrive(n, _):
             d = order(n)
-            b = block(g, d)
-            drain(b, sem_z.at[d])
-            remote(b, b, snd_y.at[d], sem_y.at[d], y_mate, z).start()
-            remote(b, b, snd_c.at[d], sem_c.at[d], c_mate, z).start()
-
-            @pl.when(takes)
-            def _():
-                x = half(d, mine)
-                drain(x, sem_x.at[d])
-                remote(x, x, snd_yx.at[d], sem_yx.at[d], y_mate, z).start()
-                remote(x, x, snd_cx.at[d], sem_cx.at[d], c_mate, z).start()
-
-        @pl.when(n > 0)
-        def _():
-            d = order(n - 1)
-            b = block(slot_y, d)
-            drain(b, sem_y.at[d])
-            remote(b, b, snd_c2.at[d], sem_c2.at[d], c_mate, z).start()
-
-            @pl.when(takes)
-            def _():
-                x = half(d, 2 * HD - mine)
-                drain(x, sem_yx.at[d])
-                remote(x, x, snd_cx2.at[d], sem_cx.at[d], c_mate, z).start()
-
-        return 0
-
-    lax.fori_loop(0, DP + 1, relay, 0)
+            drain(block(mate, d, size), sem_c.at[d])
+            drain(block(slot_cy, d, size), sem_c2.at[d])
+
+            @pl.when(jnp.logical_not(takes))
+            def _():
+                drain(block(4, d, size), sem_cx.at[d])
+
+            return 0
+
+        lax.fori_loop(0, DP, arrive, 0)
+
+        if size < ROWS:
+            lax.fori_loop(0, DP, settle_guests, 0)
+
+    @pl.when(helps)
+    def _():
+        lax.fori_loop(0, 4, pass_on, 0)
+
+    @pl.when(early)
+    def _():
+        relayout(ROWS - GUEST)
+
+    @pl.when(jnp.logical_not(early))
+    def _():
+        relayout(ROWS)
 
     drain(span.at[pl.ds(0, 2)], sem_k)
     lane = lax.broadcasted_iota(jnp.int32, (1, HD), 1)
@@ -227,19 +339,6 @@
             key_start = jnp.where(token >= start, before, key_start)
             before = start
         first_ref[e] = key_start
-
-    def arrive(n, _):
-        d = order(n)
-        drain(block(mate, d), sem_c.at[d])
-        drain(block(slot_cy, d), sem_c2.at[d])
-
-        @pl.when(jnp.logical_not(takes))
-        def _():
-            drain(block(4, d), sem_cx.at[d])
-
-        return 0
-
-    lax.fori_loop(0, DP, arrive, 0)
 
     row_own = pl.ds(pl.multiple_of(e_own * CHUNK, CHUNK), CHUNK)
     col_own = pl.ds(pl.multiple_of(cc_own * PIECE, PIECE), PIECE)
@@ -377,30 +476,54 @@
             def _():
                 drain(hnew.at[c], snd_h.at[c])
 
-        d = c
-        drain(block(g, d), snd_y.at[d])
-        drain(block(g, d), snd_c.at[d])
-        drain(block(slot_y, d), snd_c2.at[d])
-
-        @pl.when(takes)
-        def _():
-            drain(half(d, mine), snd_yx.at[d])
-            drain(half(d, mine), snd_cx.at[d])
-            drain(half(d, mine), snd_cx2.at[d])
-
-        @pl.when(d > 0)
-        def _():
-            drain(block(g, 0), sem_w.at[d])
-
         return 0
 
     lax.fori_loop(0, CHUNKS, sent, 0)
-    for m in range(2):
-        @pl.when(z != g + GROUP * m)
-        def _():
-            drain(half(0, 0), sem_w.at[DP + m])
-
-        drain(half(0, 0), sem_w.at[DP + 2 + m])
+
+    def sent_weights(size):
+        def one(d, _):
+            drain(block(g, d, size), snd_y.at[d])
+            drain(block(g, d, size), snd_c.at[d])
+            drain(block(slot_y, d, size), snd_c2.at[d])
+
+            @pl.when(takes)
+            def _():
+                drain(half(d, mine, size), snd_yx.at[d])
+                drain(half(d, mine, size), snd_cx.at[d])
+                drain(half(d, mine, size), snd_cx2.at[d])
+
+            @pl.when(d > 0)
+            def _():
+                drain(block(g, 0, size), sem_w.at[d])
+
+            return 0
+
+        lax.fori_loop(0, DP, one, 0)
+        for m in range(2):
+            @pl.when(z != g + GROUP * m)
+            def _():
+                drain(half(0, 0, size), sem_w.at[DP + m])
+
+            drain(half(0, 0, size), sem_w.at[DP + 2 + m])
+
+        if size < ROWS:
+            for n in range(2):
+                for r in range(4):
+                    drain(staged.at[n, r], snd_s.at[n, r])
+
+    @pl.when(early)
+    def _():
+        sent_weights(ROWS - GUEST)
+
+    @pl.when(jnp.logical_not(early))
+    def _():
+        sent_weights(ROWS)
+
+    @pl.when(helps)
+    def _():
+        for n in range(2):
+            for r in range(4):
+                drain(staged.at[n, r], snd_g.at[n, r])
 
     @pl.when(feeds)
     def _():
@@ -441,6 +564,8 @@
             pltpu.VMEM((CHUNKS, DP - 1, CHUNK, PIECE), bf16),
             pltpu.VMEM((CHUNKS, CHUNK, PIECE), bf16),
             pltpu.VMEM((CHUNK, WIDTH), bf16),
+            pltpu.VMEM((2, 4, GUEST, 10 * HD), bf16),
+            dma(2, 4), dma(2, 4), dma(2, 4), dma(DP), dma(DP), dma(DP),
             dma(DP + 4), dma(DP), dma(DP), dma(DP), dma(DP), dma(DP), dma(DP), dma(DP),
             dma(DP), dma(DP), dma(DP), dma(DP), dma(DP), dma(DP),
             pltpu.SemaphoreType.DMA, dma(DP - 1), dma(CHUNKS), dma(CHUNKS), dma(CHUNKS),

time: 315 us -> 289 us (0.917)
  Pallas kernels: 313 us -> 287 us
    pallas_call x1, Pallas kernels: 313 us -> 287 us  [shards(): pl.pallas_call(kernel, out_shape=jax.ShapeDtypeStruct((CHUNK, WIDTH), bf1...]
where the time goes in v4:
time: 289 us; the launch traced here: 288 us
  Pallas kernels  287 us (99%)
    pallas_call x1, Pallas kernels, shards(): pl.pallas_call(kernel, out_shape=jax.ShapeDtypeStruct((CHUNK, WIDTH), bf1...  287 us

profile of v4, /device:TPU:23, one launch (start us, length us, event | category | flops | bytes accessed | tf_op | source)
XLA Modules:
  0.0 288.5 jit_solution(9622358867275172218)
XLA Ops:
  0.0 287.0 %shard_map.46 = bf16[16,2560]{1,0:T(8,128)(2,1)} custom-call(bf16[1,128,2560]{2,1,0:T(8,128)(2,1)} %x_ref.1, s32[1,8]{1,0:T(1,128)} %sp_ref.1, bf16[1,320,3840]{2,1,0:T(8,128)(2,1)} %qkv_ref.1, bf16[1,320,1280]{2,1,0:T(8,128)(2,1)} %ow_ref.1), custom_call_target="tpu_custom_call" | custom-call | tf_op jit(solution)/shard_map/pallas_call | solution.py:543
  287.0 1.4 dynamic-slice_bitcast_fusion

commit v5 on v4

--- a/solution.py
+++ b/solution.py
@@ -21,14 +21,14 @@
 AHEAD = 2
 FAR = (0, 3, 1, 2)
 EARLY = 2
-GUEST = 112
+GUEST = 16
 MESH = pl.DeviceIdType.MESH
 
 
 def kernel(
     x_ref, sp_ref, qkv_ref, ow_ref, out_ref,
     w, hbuf, normed, qbuf, kc, vc, span, first_ref, part, sendb, rbuf, hnew, outb,
-    staged, sem_s, snd_s, snd_g, sem_gz, sem_gc, snd_gc,
+    staged, extras, sem_s, snd_s, snd_g, sem_gz, sem_gc, snd_gc,
     sem_w, sem_z, sem_x, sem_y, sem_yx, sem_c, sem_c2, sem_cx,
     snd_y, snd_yx, snd_c, snd_c2, snd_cx, snd_cx2,
     sem_k, snd_k, sem_h, snd_i, sem_r, snd_r, snd_h, sem_o, sem_f, snd_f,
@@ -139,30 +139,39 @@
             feed(2 * (layer - layers // 2) + n)
 
     def hand_over():
-        rows = pl.ds(ROWS - GUEST, GUEST)
         for r in range(4):
-            cols = pl.ds(10 * HD * r, 10 * HD)
-            src = qkv_ref.at[0, rows, cols] if r < 3 else ow_ref.at[0, rows, :]
-            for n, to_sec in enumerate((sec, y_mate)):
-                remote(
-                    src, staged.at[n, r], snd_s.at[n, r], sem_s.at[n, r], to_sec + shift, z
-                ).start()
+            for kind in range(2):
+                rows = pl.ds(ROWS - GUEST, GUEST) if kind == 0 else pl.ds(0, ROWS)
+                first, count = (0, DP * HD) if kind == 0 else (DP * HD, 2 * HD)
+                if r < 3:
+                    src = qkv_ref.at[0, rows, pl.ds(10 * HD * r + first, count)]
+                else:
+                    src = ow_ref.at[0, rows, pl.ds(first, count)]
+                for n, to_sec in enumerate((sec, y_mate)):
+                    dst = (staged if kind == 0 else extras).at[n, r]
+                    remote(
+                        src, dst, snd_s.at[kind, n, r], sem_s.at[kind, n, r], to_sec + shift, z
+                    ).start()
 
     def pass_on(r, _):
-        rows = pl.ds(pl.multiple_of(z * ROWS + ROWS - GUEST, 16), GUEST)
+        some = pl.ds(pl.multiple_of(z * ROWS + ROWS - GUEST, 16), GUEST)
+        every = pl.ds(pl.multiple_of(z * ROWS, 16), ROWS)
         cols = pl.ds(pl.multiple_of(r * HD, HD), HD)
         for n, slot in enumerate((g, slot_y)):
-            drain(staged.at[n, r], sem_s.at[n, r])
+            drain(staged.at[n, r], sem_s.at[0, n, r])
             for j in (4, 3, 5, 2, 6, 1, 7, 0):
                 to_z = (z + j) % DP
                 src = staged.at[n, r, :, pl.ds(pl.multiple_of(to_z * HD, HD), HD)]
                 remote(
-                    src, w.at[slot, rows, cols], snd_g.at[n, r], sem_gz.at[z], sec - shift, to_z
+                    src, w.at[slot, some, cols], snd_g.at[0, n, r], sem_gz.at[z],
+                    sec - shift, to_z,
                 ).start()
+        for n, slot in enumerate((g, slot_y)):
+            drain(extras.at[n, r], sem_s.at[1, n, r])
             for m in range(2):
-                src = staged.at[n, r, :, pl.ds((DP + m) * HD, HD)]
+                src = extras.at[n, r, :, pl.ds(m * HD, HD)]
                 remote(
-                    src, w.at[4, rows, cols], snd_g.at[n, r], sem_gz.at[z],
+                    src, w.at[4, every, cols], snd_g.at[1, n, r], sem_gz.at[z],
                     sec - shift, slot + GROUP * m,
                 ).start()
         return 0
@@ -173,8 +182,8 @@
 
         @pl.when(takes)
         def _():
-            drain(w.at[0, pl.ds(0, 3 * GUEST), :], sem_gz.at[z_s])
-            x = w.at[4, rows, :]
+            drain(w.at[0, pl.ds(0, 2 * GUEST + ROWS), :], sem_gz.at[z_s])
+            x = block(4, order(n), ROWS)
             remote(x, x, snd_gc.at[z_s], sem_gc.at[z_s], c_mate, z).start()
 
         @pl.when(jnp.logical_not(takes))
@@ -190,11 +199,11 @@
         @pl.when(takes)
         def _():
             drain(w.at[0, pl.ds(0, 2 * GUEST), :], sem_gc.at[z_s])
-            drain(w.at[0, pl.ds(0, 3 * GUEST), :], snd_gc.at[z_s])
+            drain(w.at[0, pl.ds(0, 2 * GUEST + ROWS), :], snd_gc.at[z_s])
 
         @pl.when(jnp.logical_not(takes))
         def _():
-            drain(w.at[0, pl.ds(0, 3 * GUEST), :], sem_gc.at[z_s])
+            drain(w.at[0, pl.ds(0, 2 * GUEST + ROWS), :], sem_gc.at[z_s])
             drain(w.at[0, pl.ds(0, 2 * GUEST), :], snd_gc.at[z_s])
 
         return 0
@@ -237,7 +246,7 @@
                 for src, dst in head:
                     remote(src, dst, sem_w.at[n], sem_z.at[d], sec, to_z).start()
 
-            @pl.when(to_z % GROUP == g)
+            @pl.when((to_z % GROUP == g) & (size == ROWS))
             def _():
                 m = to_z // GROUP
                 extra = parts(8 + m, 4)
@@ -273,7 +282,7 @@
                 remote(b, b, snd_y.at[d], sem_y.at[d], y_mate, z).start()
                 remote(b, b, snd_c.at[d], sem_c.at[d], c_mate, z).start()
 
-                @pl.when(takes)
+                @pl.when(takes & (size == ROWS))
                 def _():
                     x = half(d, mine, size)
                     drain(x, sem_x.at[d])
@@ -287,7 +296,7 @@
                 drain(b, sem_y.at[d])
                 remote(b, b, snd_c2.at[d], sem_c2.at[d], c_mate, z).start()
 
-                @pl.when(takes)
+                @pl.when(takes & (size == ROWS))
                 def _():
                     x = half(d, 2 * HD - mine, size)
                     drain(x, sem_yx.at[d])
@@ -304,7 +313,7 @@
             drain(block(mate, d, size), sem_c.at[d])
             drain(block(slot_cy, d, size), sem_c2.at[d])
 
-            @pl.when(jnp.logical_not(takes))
+            @pl.when(jnp.logical_not(takes) & (size == ROWS))
             def _():
                 drain(block(4, d, size), sem_cx.at[d])
 
@@ -380,19 +389,21 @@
         allowed = same & (key_pos <= tok_pos) & (key_pos.astype(jnp.float32) >= first)
 
         window = pl.ds(pl.multiple_of(c * CHUNK, CHUNK), KEYS)
-        attended = []
+        scores, vals = [], []
         for s in range(SLOTS):
             cols = pl.ds(s * HD, HD)
             keys = jnp.concatenate([kc[0, window, cols], kc[1, window, cols]], axis=0)
-            vals = jnp.concatenate([vc[0, window, cols], vc[1, window, cols]], axis=0)
-            scores = lax.dot_general(
+            vals.append(jnp.concatenate([vc[0, window, cols], vc[1, window, cols]], axis=0))
+            scores.append(lax.dot_general(
                 qbuf[s], keys, (((1,), (1,)), ((), ())), preferred_element_type=jnp.float32
-            ) * scale
-            weights = jnp.where(allowed, jnp.exp(scores), 0.0)
-            probs = (weights / jnp.sum(weights, axis=-1, keepdims=True)).astype(jnp.bfloat16)
-            attended.append(
-                jnp.dot(probs, vals, preferred_element_type=jnp.float32).astype(jnp.bfloat16)
-            )
+            ))
+        weights = [jnp.where(allowed, jnp.exp(x * scale), 0.0) for x in scores]
+        sums = [jnp.sum(x, axis=-1, keepdims=True) for x in weights]
+        probs = [(x / y).astype(jnp.bfloat16) for x, y in zip(weights, sums)]
+        attended = [
+            jnp.dot(x, y, preferred_element_type=jnp.float32).astype(jnp.bfloat16)
+            for x, y in zip(probs, vals)
+        ]
 
         for turn in range(GROUP):
             cc = (cc_own + FAR[turn]) % GROUP
@@ -486,7 +497,7 @@
             drain(block(g, d, size), snd_c.at[d])
             drain(block(slot_y, d, size), snd_c2.at[d])
 
-            @pl.when(takes)
+            @pl.when(takes & (size == ROWS))
             def _():
                 drain(half(d, mine, size), snd_yx.at[d])
                 drain(half(d, mine, size), snd_cx.at[d])
@@ -499,17 +510,18 @@
             return 0
 
         lax.fori_loop(0, DP, one, 0)
-        for m in range(2):
-            @pl.when(z != g + GROUP * m)
-            def _():
-                drain(half(0, 0, size), sem_w.at[DP + m])
-
-            drain(half(0, 0, size), sem_w.at[DP + 2 + m])
-
-        if size < ROWS:
+        if size == ROWS:
+            for m in range(2):
+                @pl.when(z != g + GROUP * m)
+                def _():
+                    drain(half(0, 0, size), sem_w.at[DP + m])
+
+                drain(half(0, 0, size), sem_w.at[DP + 2 + m])
+        else:
             for n in range(2):
                 for r in range(4):
-                    drain(staged.at[n, r], snd_s.at[n, r])
+                    drain(staged.at[n, r], snd_s.at[0, n, r])
+                    drain(extras.at[n, r], snd_s.at[1, n, r])
 
     @pl.when(early)
     def _():
@@ -523,7 +535,8 @@
     def _():
         for n in range(2):
             for r in range(4):
-                drain(staged.at[n, r], snd_g.at[n, r])
+                drain(staged.at[n, r], snd_g.at[0, n, r])
+                drain(extras.at[n, r], snd_g.at[1, n, r])
 
     @pl.when(feeds)
     def _():
@@ -564,8 +577,9 @@
             pltpu.VMEM((CHUNKS, DP - 1, CHUNK, PIECE), bf16),
             pltpu.VMEM((CHUNKS, CHUNK, PIECE), bf16),
             pltpu.VMEM((CHUNK, WIDTH), bf16),
-            pltpu.VMEM((2, 4, GUEST, 10 * HD), bf16),
-            dma(2, 4), dma(2, 4), dma(2, 4), dma(DP), dma(DP), dma(DP),
+            pltpu.VMEM((2, 4, GUEST, DP * HD), bf16),
+            pltpu.VMEM((2, 4, ROWS, 2 * HD), bf16),
+            dma(2, 2, 4), dma(2, 2, 4), dma(2, 2, 4), dma(DP), dma(DP), dma(DP),
             dma(DP + 4), dma(DP), dma(DP), dma(DP), dma(DP), dma(DP), dma(DP), dma(DP),
             dma(DP), dma(DP), dma(DP), dma(DP), dma(DP), dma(DP),
             pltpu.SemaphoreType.DMA, dma(DP - 1), dma(CHUNKS), dma(CHUNKS), dma(CHUNKS),

time: 289 us -> 278 us (0.962)
  Pallas kernels: 287 us -> 276 us
    pallas_call x1, Pallas kernels: 287 us -> 276 us  [shards(): pl.pallas_call(kernel, out_shape=jax.ShapeDtypeStruct((CHUNK, WIDTH), bf1...]
where the time goes in v5:
time: 278 us; the launch traced here: 277 us
  Pallas kernels  276 us (99%)
    pallas_call x1, Pallas kernels, shards(): pl.pallas_call(kernel, out_shape=jax.ShapeDtypeStruct((CHUNK, WIDTH), bf1...  276 us

profile of v5, /device:TPU:23, one launch (start us, length us, event | category | flops | bytes accessed | tf_op | source)
XLA Modules:
  0.0 277.4 jit_solution(10186733015465674342)
XLA Ops:
  0.0 276.0 %shard_map.46 = bf16[16,2560]{1,0:T(8,128)(2,1)} custom-call(bf16[1,128,2560]{2,1,0:T(8,128)(2,1)} %x_ref.1, s32[1,8]{1,0:T(1,128)} %sp_ref.1, bf16[1,320,3840]{2,1,0:T(8,128)(2,1)} %qkv_ref.1, bf16[1,320,1280]{2,1,0:T(8,128)(2,1)} %ow_ref.1), custom_call_target="tpu_custom_call" | custom-call | tf_op jit(solution)/shard_map/pallas_call | solution.py:556
  276.0 1.4 dynamic-slice_bitcast_fusion

commit v6 on v5

--- a/solution.py
+++ b/solution.py
@@ -56,7 +56,10 @@
     e_own = z // GROUP
     cc_own = z % GROUP
     out_z = GROUP * e_own + 2 * (q % 2) + q // 2
-    is_out = (out_z == z) & (cc_own == g)
+    is_out = out_z == z
+    next_sec = base + GROUP + slot_y
+    peers = [(z + d) % DP for d in range(DP)]
+    peer_rows = [pl.ds(pl.multiple_of(p // GROUP * CHUNK, CHUNK), CHUNK) for p in peers]
 
     early = layer < EARLY
     helps = layer >= layers - EARLY
@@ -105,19 +108,28 @@
                 greet((layers // 2 + n) * GROUP + g, 4 * e + 2 * (g % 2) + g // 2)
 
     g_out = (q_z + 2 * ((layers - 1) % 2)) % GROUP
-    from_sec, from_z = sections - GROUP + g_out, e_z * GROUP + g
-    greet(base + GROUP - 1 - g, z)
-
-    @pl.when((from_sec != sec) | (from_z != z))
-    def _():
-        greet(from_sec, from_z)
+    from_sec = sections - GROUP + g_out
+
+    @pl.when(jnp.logical_not(last))
+    def _():
+        greet(base + GROUP - 1 - g, z)
+        greet(from_sec, e_z * GROUP + g)
+
+    @pl.when(last)
+    def _():
+        for cc in range(GROUP):
+            from_z = e_z * GROUP + cc
+
+            @pl.when((from_sec != sec) | (from_z != z))
+            def _():
+                greet(from_sec, from_z)
 
     kc[:, pl.ds(0, BACK), :] = jnp.zeros((2, BACK, SLOTS * HD), jnp.bfloat16)
     vc[:, pl.ds(0, BACK), :] = jnp.zeros((2, BACK, SLOTS * HD), jnp.bfloat16)
     span[2] = jnp.zeros((8, HD), jnp.int32)
     span[2, pl.ds(0, 1), pl.ds(0, SPANS)] = sp_ref[...]
 
-    partners = 2 * DP + 1 + jnp.where(last, layers - is_out.astype(jnp.int32), DP)
+    partners = 2 * DP + jnp.where(last, layers - 1 + GROUP - is_out.astype(jnp.int32), DP + 1)
     partners += DP * feeds.astype(jnp.int32) + 2 * early.astype(jnp.int32)
     pl.semaphore_wait(barrier, partners + DP * helps.astype(jnp.int32))
 
@@ -264,10 +276,10 @@
                 for src, dst in extra[2:]:
                     remote(src, dst, sem_w.at[DP + 2 + m], sem_x.at[d], y_mate, to_z).start()
 
+        for n in range(AHEAD):
+            send_round(n)
         if size < ROWS:
             hand_over()
-        for n in range(AHEAD):
-            send_round(n)
 
         def relay(n, _):
             @pl.when(n + AHEAD < DP)
@@ -419,19 +431,18 @@
                 )
                 total = term if total is None else total + term
             cols = pl.ds(pl.multiple_of(cc * PIECE, PIECE), PIECE)
-            part[:, cols] = total
+            if turn == 0:
+                part[...] = total
             sendb[c, :, cols] = total.astype(jnp.bfloat16)
             for d in ((FAR[turn] + GROUP), FAR[turn]):
                 if d > 0:
-                    to_z = (z + d) % DP
-                    rows = pl.ds(pl.multiple_of(to_z // GROUP * CHUNK, CHUNK), CHUNK)
                     remote(
-                        sendb.at[c, rows, cols], rbuf.at[c, d - 1],
-                        snd_r.at[c], sem_r.at[c], sec, to_z,
+                        sendb.at[c, peer_rows[d], cols], rbuf.at[c, d - 1],
+                        snd_r.at[c], sem_r.at[c], sec, peers[d],
                     ).start()
 
     def combine(c):
-        total = part[row_own, col_own] + hbuf[c, row_own, col_own].astype(jnp.float32)
+        total = part[row_own, :] + hbuf[c, row_own, col_own].astype(jnp.float32)
         drain(rbuf.at[c], sem_r.at[c])
         for d in range(DP - 1):
             total = total + rbuf[c, d].astype(jnp.float32)
@@ -442,21 +453,29 @@
             for n in (4, 3, 5, 2, 6, 1, 7, 0):
                 remote(
                     hnew.at[c], hbuf.at[c, row_own, col_own],
-                    snd_h.at[c], sem_h.at[c], base + GROUP + slot_y, (z + n) % DP,
+                    snd_h.at[c], sem_h.at[c], next_sec, peers[n],
                 ).start()
 
-        @pl.when(last)
+        @pl.when(last & (c < CHUNKS - 1))
         def _():
             to_sec = c * GROUP + cc_own
-            here = (to_sec == sec) & is_out
-
-            @pl.when(here)
-            def _():
-                pltpu.make_async_copy(hnew.at[c], outb.at[:, col_own], sem_o).start()
-
-            @pl.when(jnp.logical_not(here))
-            def _():
-                remote(hnew.at[c], outb.at[:, col_own], snd_h.at[c], sem_o, to_sec, out_z).start()
+            remote(hnew.at[c], outb.at[:, col_own], snd_h.at[c], sem_o, to_sec, out_z).start()
+
+        @pl.when(last & (c == CHUNKS - 1))
+        def _():
+            for n in range(GROUP):
+                here = (n == g) & is_out
+
+                @pl.when(here)
+                def _():
+                    pltpu.make_async_copy(hnew.at[c], outb.at[:, col_own], sem_o).start()
+
+                @pl.when(jnp.logical_not(here))
+                def _():
+                    to_sec = sections - GROUP + n
+                    remote(
+                        hnew.at[c], outb.at[:, col_own], snd_h.at[c], sem_o, to_sec, out_z
+                    ).start()
 
     def step(c, _):
         project(c)
@@ -467,12 +486,20 @@
     lax.fori_loop(0, CHUNKS, step, 0)
 
     result = outb.at[:, pl.ds(pl.multiple_of(g * PIECE, PIECE), PIECE)]
-    drain(result, sem_o)
-    for to_sec in (c_mate, y_mate, base + GROUP - 1 - g):
-        remote(result, result, snd_f, sem_f, to_sec, z).start()
-    drain(outb.at[:, pl.ds(0, 3 * PIECE)], sem_f)
+
+    @pl.when(jnp.logical_not(last))
+    def _():
+        drain(result, sem_o)
+        for to_sec in (c_mate, y_mate, base + GROUP - 1 - g):
+            remote(result, result, snd_f, sem_f, to_sec, z).start()
+        drain(outb.at[:, pl.ds(0, 3 * PIECE)], sem_f)
+        drain(outb.at[:, pl.ds(0, 3 * PIECE)], snd_f)
+
+    @pl.when(last)
+    def _():
+        drain(outb, sem_o)
+
     out_ref[...] = outb[...]
-    drain(outb.at[:, pl.ds(0, 3 * PIECE)], snd_f)
 
     def sent(c, _):
         drain(rbuf.at[c], snd_r.at[c])
@@ -483,9 +510,17 @@
 
         @pl.when(last)
         def _():
-            @pl.when((c != layer) | jnp.logical_not(is_out))
+            @pl.when(c < CHUNKS - 1)
             def _():
                 drain(hnew.at[c], snd_h.at[c])
+
+            @pl.when((c == CHUNKS - 1) & is_out)
+            def _():
+                drain(outb.at[:, pl.ds(0, 3 * PIECE)], snd_h.at[c])
+
+            @pl.when((c == CHUNKS - 1) & jnp.logical_not(is_out))
+            def _():
+                drain(outb, snd_h.at[c])
 
         return 0
 
@@ -572,7 +607,7 @@
             pltpu.VMEM((2, LEN + BACK, SLOTS * HD), bf16),
             pltpu.VMEM((3, 8, HD), jnp.int32),
             pltpu.VMEM((2, LEN, HD), jnp.float32),
-            pltpu.VMEM((2 * CHUNK, WIDTH), jnp.float32),
+            pltpu.VMEM((2 * CHUNK, PIECE), jnp.float32),
             pltpu.VMEM((CHUNKS, 2 * CHUNK, WIDTH), bf16),
             pltpu.VMEM((CHUNKS, DP - 1, CHUNK, PIECE), bf16),
             pltpu.VMEM((CHUNKS, CHUNK, PIECE), bf16),

time: 278 us -> 275 us (0.989)
  Pallas kernels: 276 us -> 273 us
    pallas_call x1, Pallas kernels: 276 us -> 273 us  [shards(): pl.pallas_call(kernel, out_shape=jax.ShapeDtypeStruct((CHUNK, WIDTH), bf1...]
where the time goes in v6:
time: 275 us
  Pallas kernels  273 us (99%)
    pallas_call x1, Pallas kernels, shards(): pl.pallas_call(kernel, out_shape=jax.ShapeDtypeStruct((CHUNK, WIDTH), bf1...  273 us

profile of v6, /device:TPU:23, one launch (start us, length us, event | category | flops | bytes accessed | tf_op | source)
XLA Modules:
  0.0 274.5 jit_solution(18228840116741069632)
XLA Ops:
  0.0 273.1 %shard_map.46 = bf16[16,2560]{1,0:T(8,128)(2,1)} custom-call(bf16[1,128,2560]{2,1,0:T(8,128)(2,1)} %x_ref.1, s32[1,8]{1,0:T(1,128)} %sp_ref.1, bf16[1,320,3840]{2,1,0:T(8,128)(2,1)} %qkv_ref.1, bf16[1,320,1280]{2,1,0:T(8,128)(2,1)} %ow_ref.1), custom_call_target="tpu_custom_call" | custom-call | tf_op jit(solution)/shard_map/pallas_call | solution.py:591
  273.1 1.4 dynamic-slice_bitcast_fusion

commit v7 on v6

--- a/solution.py
+++ b/solution.py
@@ -27,7 +27,7 @@
 
 def kernel(
     x_ref, sp_ref, qkv_ref, ow_ref, out_ref,
-    w, hbuf, normed, qbuf, kc, vc, span, first_ref, part, sendb, rbuf, hnew, outb,
+    w, hbuf, normed, qbuf, kc, vc, span, first_ref, mask_ref, part, sendb, rbuf, hnew, outb,
     staged, extras, sem_s, snd_s, snd_g, sem_gz, sem_gc, snd_gc,
     sem_w, sem_z, sem_x, sem_y, sem_yx, sem_c, sem_c2, sem_cx,
     snd_y, snd_yx, snd_c, snd_c2, snd_cx, snd_cx2,
@@ -233,6 +233,34 @@
         rows = pl.ds(pl.multiple_of((z + DP - d) % DP * ROWS, ROWS), size)
         return w.at[4, rows, pl.ds(pl.multiple_of(at, 2 * HD), 2 * HD)]
 
+    def prepare():
+        drain(span.at[pl.ds(0, 2)], sem_k)
+        lane = lax.broadcasted_iota(jnp.int32, (1, HD), 1)
+        token = lax.broadcasted_iota(jnp.int32, (LEN, HD), 0).astype(jnp.float32)
+        for e in range(2):
+            lens = span[e, pl.ds(0, 1), :].astype(jnp.float32)
+            key_start = jnp.zeros((LEN, HD), jnp.float32)
+            before = jnp.zeros((1, 1), jnp.float32)
+            for s in range(1, SPANS):
+                start = jnp.sum(jnp.where(lane < s, lens, 0.0), axis=1, keepdims=True)
+                key_start = jnp.where(token >= start, before, key_start)
+                before = start
+            first_ref[e] = key_start
+
+        def mask(c, _):
+            tok = pl.ds(pl.multiple_of(c * CHUNK, CHUNK), CHUNK)
+            first = jnp.concatenate([first_ref[0, tok, :], first_ref[1, tok, :]], axis=0)
+            row = lax.broadcasted_iota(jnp.int32, (2 * CHUNK, 2 * KEYS), 0)
+            col = lax.broadcasted_iota(jnp.int32, (2 * CHUNK, 2 * KEYS), 1)
+            same = (row < CHUNK) == (col < KEYS)
+            key_pos = c * CHUNK - BACK + jnp.where(col < KEYS, col, col - KEYS)
+            tok_pos = c * CHUNK + jnp.where(row < CHUNK, row, row - CHUNK)
+            allowed = same & (key_pos <= tok_pos) & (key_pos.astype(jnp.float32) >= first)
+            mask_ref[c] = allowed.astype(jnp.float32)
+            return 0
+
+        lax.fori_loop(0, CHUNKS, mask, 0)
+
     def relayout(size):
         def parts(i, slot):
             rows = pl.ds(pl.multiple_of(z * ROWS, ROWS), size)
@@ -276,15 +304,16 @@
                 for src, dst in extra[2:]:
                     remote(src, dst, sem_w.at[DP + 2 + m], sem_x.at[d], y_mate, to_z).start()
 
-        for n in range(AHEAD):
+        ahead = 3 if size < ROWS else AHEAD
+        for n in range(ahead):
             send_round(n)
         if size < ROWS:
             hand_over()
 
         def relay(n, _):
-            @pl.when(n + AHEAD < DP)
-            def _():
-                send_round(n + AHEAD)
+            @pl.when(n + ahead < DP)
+            def _():
+                send_round(n + ahead)
 
             @pl.when(n < DP)
             def _():
@@ -317,6 +346,7 @@
             return 0
 
         lax.fori_loop(0, DP + 1, relay, 0)
+        prepare()
         if size < ROWS:
             lax.fori_loop(0, DP, take_guests, 0)
 
@@ -347,19 +377,6 @@
     @pl.when(jnp.logical_not(early))
     def _():
         relayout(ROWS)
-
-    drain(span.at[pl.ds(0, 2)], sem_k)
-    lane = lax.broadcasted_iota(jnp.int32, (1, HD), 1)
-    token = lax.broadcasted_iota(jnp.int32, (LEN, HD), 0).astype(jnp.float32)
-    for e in range(2):
-        lens = span[e, pl.ds(0, 1), :].astype(jnp.float32)
-        key_start = jnp.zeros((LEN, HD), jnp.float32)
-        before = jnp.zeros((1, 1), jnp.float32)
-        for s in range(1, SPANS):
-            start = jnp.sum(jnp.where(lane < s, lens, 0.0), axis=1, keepdims=True)
-            key_start = jnp.where(token >= start, before, key_start)
-            before = start
-        first_ref[e] = key_start
 
     row_own = pl.ds(pl.multiple_of(e_own * CHUNK, CHUNK), CHUNK)
     col_own = pl.ds(pl.multiple_of(cc_own * PIECE, PIECE), PIECE)
@@ -391,15 +408,7 @@
             vc[1, new, pl.ds(s * HD, n * HD)] = v[CHUNK:]
 
     def attend(c):
-        tok = pl.ds(pl.multiple_of(c * CHUNK, CHUNK), CHUNK)
-        first = jnp.concatenate([first_ref[0, tok, :], first_ref[1, tok, :]], axis=0)
-        row = lax.broadcasted_iota(jnp.int32, (2 * CHUNK, 2 * KEYS), 0)
-        col = lax.broadcasted_iota(jnp.int32, (2 * CHUNK, 2 * KEYS), 1)
-        same = (row < CHUNK) == (col < KEYS)
-        key_pos = c * CHUNK - BACK + jnp.where(col < KEYS, col, col - KEYS)
-        tok_pos = c * CHUNK + jnp.where(row < CHUNK, row, row - CHUNK)
-        allowed = same & (key_pos <= tok_pos) & (key_pos.astype(jnp.float32) >= first)
-
+        allowed = mask_ref[c] > 0.0
         window = pl.ds(pl.multiple_of(c * CHUNK, CHUNK), KEYS)
         scores, vals = [], []
         for s in range(SLOTS):
@@ -607,6 +616,7 @@
             pltpu.VMEM((2, LEN + BACK, SLOTS * HD), bf16),
             pltpu.VMEM((3, 8, HD), jnp.int32),
             pltpu.VMEM((2, LEN, HD), jnp.float32),
+            pltpu.VMEM((CHUNKS, 2 * CHUNK, 2 * KEYS), jnp.float32),
             pltpu.VMEM((2 * CHUNK, PIECE), jnp.float32),
             pltpu.VMEM((CHUNKS, 2 * CHUNK, WIDTH), bf16),
             pltpu.VMEM((CHUNKS, DP - 1, CHUNK, PIECE), bf16),

time: 275 us -> 273 us (level)
  no operation moved by 1% of the time
where the time goes in v7:
time: 273 us
  Pallas kernels  272 us (100%)
    pallas_call x1, Pallas kernels, shards(): pl.pallas_call(kernel, out_shape=jax.ShapeDtypeStruct((CHUNK, WIDTH), bf1...  272 us

profile of v7, /device:TPU:23, one launch (start us, length us, event | category | flops | bytes accessed | tf_op | source)
XLA Modules:
  0.0 273.0 jit_solution(17188351977031329758)
XLA Ops:
  0.0 271.5 %shard_map.46 = bf16[16,2560]{1,0:T(8,128)(2,1)} custom-call(bf16[1,128,2560]{2,1,0:T(8,128)(2,1)} %x_ref.1, s32[1,8]{1,0:T(1,128)} %sp_ref.1, bf16[1,320,3840]{2,1,0:T(8,128)(2,1)} %qkv_ref.1, bf16[1,320,1280]{2,1,0:T(8,128)(2,1)} %ow_ref.1), custom_call_target="tpu_custom_call" | custom-call | tf_op jit(solution)/shard_map/pallas_call | solution.py:600
  271.6 1.4 dynamic-slice_bitcast_fusion

commit v8 on v7

--- a/solution.py
+++ b/solution.py
@@ -18,7 +18,7 @@
 BACK = 48
 KEYS = BACK + CHUNK
 PIECE = 640
-AHEAD = 2
+AHEAD = 3
 FAR = (0, 3, 1, 2)
 EARLY = 2
 GUEST = 16
@@ -304,17 +304,13 @@
                 for src, dst in extra[2:]:
                     remote(src, dst, sem_w.at[DP + 2 + m], sem_x.at[d], y_mate, to_z).start()
 
-        ahead = 3 if size < ROWS else AHEAD
+        ahead = 4 if size < ROWS else AHEAD
         for n in range(ahead):
             send_round(n)
         if size < ROWS:
             hand_over()
 
         def relay(n, _):
-            @pl.when(n + ahead < DP)
-            def _():
-                send_round(n + ahead)
-
             @pl.when(n < DP)
             def _():
                 d = order(n)
@@ -329,6 +325,10 @@
                     drain(x, sem_x.at[d])
                     remote(x, x, snd_yx.at[d], sem_yx.at[d], y_mate, z).start()
                     remote(x, x, snd_cx.at[d], sem_cx.at[d], c_mate, z).start()
+
+            @pl.when(n + ahead < DP)
+            def _():
+                send_round(n + ahead)
 
             @pl.when(n > 0)
             def _():

time: 273 us -> 280 us (1.026)
  Pallas kernels: 272 us -> 278 us
    pallas_call x1, Pallas kernels: 272 us -> 278 us  [shards(): pl.pallas_call(kernel, out_shape=jax.ShapeDtypeStruct((CHUNK, WIDTH), bf1...]
where the time goes in v8:
time: 280 us
  Pallas kernels  278 us (99%)
    pallas_call x1, Pallas kernels, shards(): pl.pallas_call(kernel, out_shape=jax.ShapeDtypeStruct((CHUNK, WIDTH), bf1...  278 us

profile of v8, /device:TPU:23, one launch (start us, length us, event | category | flops | bytes accessed | tf_op | source)
XLA Modules:
  0.0 279.7 jit_solution(2564888816651938946)
XLA Ops:
  0.0 278.3 %shard_map.46 = bf16[16,2560]{1,0:T(8,128)(2,1)} custom-call(bf16[1,128,2560]{2,1,0:T(8,128)(2,1)} %x_ref.1, s32[1,8]{1,0:T(1,128)} %sp_ref.1, bf16[1,320,3840]{2,1,0:T(8,128)(2,1)} %qkv_ref.1, bf16[1,320,1280]{2,1,0:T(8,128)(2,1)} %ow_ref.1), custom_call_target="tpu_custom_call" | custom-call | tf_op jit(solution)/shard_map/pallas_call | solution.py:600
  278.3 1.4 dynamic-slice_bitcast_fusion
